TPU v7x, 512 devices: a whole 4x8x8 slice. The times are simulated.
512 devices in a mesh: enc: 16 (over y, core), row: 32 (over x, z).
Axes of the slice: x: 4, y: 8, z: 8, core: 2. Of those that a mesh axis runs over, the one named last changes fastest.
Arguments:
- patches: bfloat16 [131072, 1280], P(('enc', 'row'))
- norm_gain: float32 [1280], replicated, may hold values from 0.1 to 1.9
- merge_gain: float32 [1280], replicated, may hold values from 0.1 to 1.9
- qkv_weight: bfloat16 [1280, 1920], P('row')
- out_weight: bfloat16 [640, 1280], P('row'), may hold values from -0.25 to 0.25
- window_phase: int32 [16], replicated, may hold values from 1 to 63, as said below
- owner_enc: int32 [32768], P(('enc', 'row')), may hold values from 0 to 15, as said below
- owner_slot: int32 [32768], P(('enc', 'row')), may hold values from 0 to 4, as said below
- llm_grads: bfloat16 [40960, 5120], P(('enc', 'row')), may hold values from -6 to 6
Outputs:
- llm_inputs: bfloat16 [40960, 5120], P(('enc', 'row'))
- patch_grads: bfloat16 [131072, 1280], P(('enc', 'row'))
Inputs may be any that keep to these rules, and one draw needn't show every extreme that they name: `window_phase`: some region has phase 1 and another has 63. `owner_enc`: the owner of a merged token lies at the same index along row as its source device. A source device sends at most 5 merged tokens to one owner, and in every index along row one owner receives exactly 5 from every source. `owner_slot`: merged tokens of one source that share an owner have distinct slots.
All inputs are finite; a program needn't handle non-finite values.
Results may differ from a plain program's by a relative error of at most 0.012.
Values may be sent and summed in bfloat16 or wider, within the bound.
A program may use at most 64 MiB of HBM per device.

v0:
```python
import jax
import jax.numpy as jnp
from jax import lax
from jax.sharding import PartitionSpec as P

HEADS = 8
HEAD_DIM = 80
WIN = 64


EPS = 1e-06


def padded(block, sides, width):
    for axis, dim in sides:
        count = lax.axis_size(axis)
        forward = [(i, i + 1) for i in range(count - 1)]
        backward = [(target, source) for source, target in forward]
        low = lax.ppermute(
            lax.slice_in_dim(block, block.shape[dim] - width, None, axis=dim), axis, forward
        )
        high = lax.ppermute(lax.slice_in_dim(block, 0, width, axis=dim), axis, backward)
        block = jnp.concatenate([low, block, high], axis=dim)
    return block


def rms_norm(values, gain_vec):
    wide = values.astype(jnp.float32)
    inv_rms = lax.rsqrt(jnp.mean(wide * wide, -1, keepdims=True) + EPS)
    return (wide * inv_rms * gain_vec).astype(jnp.bfloat16)


def rms_back(values, gain_vec, upstream_in):
    wide = values.astype(jnp.float32)
    inv_rms = lax.rsqrt(jnp.mean(wide * wide, -1, keepdims=True) + EPS)
    upstream = upstream_in * gain_vec
    inner = jnp.mean(upstream * wide, -1, keepdims=True)
    return inv_rms * upstream - wide * (inv_rms * inv_rms * inv_rms) * inner


def pad_rows(values):
    padding = jnp.zeros((WIN,) + values.shape[1:], values.dtype)
    return jnp.concatenate([padding, values, padding], 0)


def key_mask(grid_phase, first_pos, group_total, count):
    positions = first_pos + jnp.arange(count, dtype=jnp.int32) + grid_phase - WIN
    valid = jnp.logical_and(positions >= 0, positions < group_total)
    return valid.reshape(count // WIN, WIN)


def aligned_set(qkv, kv_ext, grid_phase, row_count, proj_width):
    q_al = lax.dynamic_slice_in_dim(pad_rows(qkv[:, :proj_width]), grid_phase, row_count + WIN, 0)
    kv_al = lax.dynamic_slice_in_dim(kv_ext, grid_phase, row_count + WIN, 0)
    return (q_al, kv_al[:, :proj_width], kv_al[:, proj_width:])


def window_forward(q_al, k_al, v_al, key_valid):
    windows = q_al.shape[0] // WIN
    shape_four = (windows, WIN, HEADS, HEAD_DIM)
    scores = jnp.einsum(
        "wqhd,wkhd->whqk",
        q_al.reshape(shape_four),
        k_al.reshape(shape_four),
        preferred_element_type=jnp.float32,
    ) * HEAD_DIM ** (-0.5)
    scores = jnp.where(key_valid[:, None, None, :], scores, -1e30)
    highest = jnp.max(scores, -1, keepdims=True)
    expo = jnp.exp(scores - highest)
    soft_w = expo / jnp.sum(expo, -1, keepdims=True)
    soft_b = soft_w.astype(jnp.bfloat16)
    mixed = jnp.einsum(
        "whqk,wkhd->wqhd", soft_b, v_al.reshape(shape_four), preferred_element_type=jnp.float32
    )
    return (mixed.astype(jnp.bfloat16).reshape(windows * WIN, HEADS * HEAD_DIM), soft_w, soft_b)


def window_backward(q_al, k_al, v_al, soft_w, soft_b, grad_al):
    windows = q_al.shape[0] // WIN
    shape_four = (windows, WIN, HEADS, HEAD_DIM)
    q_four = q_al.reshape(shape_four)
    k_four = k_al.reshape(shape_four)
    grad_four = grad_al.reshape(shape_four)
    prob_grad = jnp.einsum(
        "wqhd,wkhd->whqk", grad_four, v_al.reshape(shape_four), preferred_element_type=jnp.float32
    )
    centred = prob_grad - jnp.sum(soft_w * prob_grad, -1, keepdims=True)
    score_grad = (soft_w * centred * HEAD_DIM ** (-0.5)).astype(jnp.bfloat16)
    dq_four = jnp.einsum("whqk,wkhd->wqhd", score_grad, k_four, preferred_element_type=jnp.float32)
    dk_four = jnp.einsum("whqk,wqhd->wkhd", score_grad, q_four, preferred_element_type=jnp.float32)
    dv_four = jnp.einsum("whqk,wqhd->wkhd", soft_b, grad_four, preferred_element_type=jnp.float32)
    flat = (windows * WIN, HEADS * HEAD_DIM)
    return (dq_four.reshape(flat), dk_four.reshape(flat), dv_four.reshape(flat))


def per_device(
    patches,
    norm_gain,
    merge_gain,
    qkv_weight,
    out_weight,
    window_phase,
    owner_enc,
    owner_slot,
    llm_grads,
):
    row_count = patches.shape[0]
    feature_width = patches.shape[1]
    proj_width = HEADS * HEAD_DIM
    row_devices = lax.axis_size("row")
    enc_devices = lax.axis_size("enc")
    grid_phase = lax.dynamic_index_in_dim(window_phase, lax.axis_index("enc"), 0, keepdims=False)
    first_pos = lax.axis_index("row") * row_count
    key_valid = key_mask(grid_phase, first_pos, row_count * row_devices, row_count + WIN)
    hidden_in = rms_norm(patches, norm_gain)
    columns = hidden_in
    qkv = jnp.dot(
        columns,
        lax.all_gather(qkv_weight, "row", axis=0, tiled=True),
        preferred_element_type=jnp.float32,
    ).astype(jnp.bfloat16)
    kv_ext = padded(qkv[:, proj_width:], (("row", 0),), WIN)
    q_al, k_al, v_al = aligned_set(qkv, kv_ext, grid_phase, row_count, proj_width)
    mixed_al, soft_w, soft_b = window_forward(q_al, k_al, v_al, key_valid)
    attended = lax.dynamic_slice_in_dim(mixed_al, WIN - grid_phase, row_count, 0)
    columns = attended
    branch = jnp.dot(
        columns,
        lax.all_gather(out_weight, "row", axis=0, tiled=True),
        preferred_element_type=jnp.float32,
    )
    resid = (patches.astype(jnp.float32) + branch).astype(jnp.bfloat16)
    normed = rms_norm(resid, merge_gain)
    merged = normed.reshape(row_count // 4, 4 * feature_width)
    slot_cap = llm_grads.shape[0] // enc_devices
    bucket_index = owner_enc * slot_cap + owner_slot
    selector = (
        bucket_index[:, None] == jnp.arange(enc_devices * slot_cap, dtype=jnp.int32)[None, :]
    ).astype(jnp.bfloat16)
    buckets = lax.dot_general(
        selector, merged, (((0,), (0,)), ((), ())), preferred_element_type=jnp.float32
    ).astype(jnp.bfloat16)
    received = lax.all_to_all(
        buckets.reshape(enc_devices, slot_cap, 4 * feature_width),
        "enc",
        split_axis=0,
        concat_axis=0,
        tiled=True,
    )
    llm_inputs = received.reshape(enc_devices * slot_cap, 4 * feature_width)
    returned = lax.all_to_all(
        llm_grads.reshape(enc_devices, slot_cap, 4 * feature_width),
        "enc",
        split_axis=0,
        concat_axis=0,
        tiled=True,
    )
    merged_grad = jnp.dot(
        selector,
        returned.reshape(enc_devices * slot_cap, 4 * feature_width),
        preferred_element_type=jnp.float32,
    )
    normed_grad = merged_grad.reshape(row_count, feature_width)
    back_qkv, back_out = (
        lax.all_gather(qkv_weight, "row", axis=0, tiled=True),
        lax.all_gather(out_weight, "row", axis=0, tiled=True),
    )
    qkv_again = jnp.dot(hidden_in, back_qkv, preferred_element_type=jnp.float32).astype(
        jnp.bfloat16
    )
    kv_again = padded(qkv_again[:, proj_width:], (("row", 0),), WIN)
    q_back, k_back, v_back = aligned_set(qkv_again, kv_again, grid_phase, row_count, proj_width)
    mixed_again, soft_back, soft_back_b = window_forward(q_back, k_back, v_back, key_valid)
    resid_grad = rms_back(resid, merge_gain, normed_grad)
    attended_grad = lax.dot_general(
        resid_grad.astype(jnp.bfloat16),
        back_out,
        (((1,), (1,)), ((), ())),
        preferred_element_type=jnp.float32,
    ).astype(jnp.bfloat16)
    grad_al = lax.dynamic_slice_in_dim(pad_rows(attended_grad), grid_phase, row_count + WIN, 0)
    dq_al, dk_al, dv_al = window_backward(q_back, k_back, v_back, soft_back, soft_back_b, grad_al)
    query_grad = lax.dynamic_slice_in_dim(dq_al, WIN - grid_phase, row_count, 0)
    kv_grad_al = jnp.concatenate([dk_al, dv_al], 1)
    kv_grad_ext = lax.dynamic_update_slice_in_dim(
        jnp.zeros((row_count + 2 * WIN, 2 * proj_width), jnp.float32), kv_grad_al, grid_phase, 0
    )
    rim_rows = jnp.concatenate([kv_grad_ext[:WIN], kv_grad_ext[row_count + WIN :]], 0)
    rims_back = padded(rim_rows, (("row", 0),), WIN)
    kv_grad = kv_grad_ext[WIN : row_count + WIN]
    kv_grad = kv_grad.at[:WIN].add(rims_back[:WIN]).at[row_count - WIN :].add(rims_back[3 * WIN :])
    qkv_grad = jnp.concatenate([query_grad, kv_grad], 1).astype(jnp.bfloat16)
    hidden_grad = lax.dot_general(
        qkv_grad, back_qkv, (((1,), (1,)), ((), ())), preferred_element_type=jnp.float32
    )
    patch_grads = (resid_grad + rms_back(patches, norm_gain, hidden_grad)).astype(jnp.bfloat16)
    return (llm_inputs, patch_grads)


def solution(mesh):
    in_specs = (
        P(("enc", "row"), None),
        P(),
        P(),
        P("row", None),
        P("row", None),
        P(),
        P(("enc", "row")),
        P(("enc", "row")),
        P(("enc", "row"), None),
    )
    out_specs = (P(("enc", "row"), None), P(("enc", "row"), None))
    return jax.shard_map(
        per_device, mesh=mesh, in_specs=in_specs, out_specs=out_specs, check_vma=False
    )
```

profile of v0, /device:TPU:1, one launch (start us, length us, event | category | flops | bytes accessed | tf_op | source)
XLA Modules:
  0.0 322.1 jit_solution(51396691314205205)
XLA Ops:
  8.6 2.3 reshape.162
  10.9 10.5 %all-to-all-start.1 = ((bf16[16,5,5120]{2,1,0:T(8,128)(2,1)}), bf16[16,5,5120]{2,1,0:T(8,128)(2,1)S(1)}, u32[]{:S(2)}, u32[]{:S(2)}) async-start(bf16[16,5,5120]{2,1,0:T(8,128)(2,1)} %reshape.162), calls=%async_computation.1 | async-start | bytes 2621440 | tf_op jit(solution)/shard_map/all_to_all | solution.py:151
  26.2 28.5 %all-to-all-done.1 = bf16[16,5,5120]{2,1,0:T(8,128)(2,1)S(1)} async-done(((bf16[16,5,5120]{2,1,0:T(8,128)(2,1)}), bf16[16,5,5120]{2,1,0:T(8,128)(2,1)S(1)}, u32[]{:S(2)}, u32[]{:S(2)}) %all-to-all-start.1) | async-done | bytes 819232 | tf_op jit(solution)/shard_map/all_to_all | solution.py:151
  55.1 49.3 %all-gather.4.cloned.1.call-done = bf16[1280,1920]{1,0:T(8,128)(2,1)} async-done(((bf16[40,1920]{1,0:T(8,128)(2,1)}), bf16[1280,1920]{1,0:T(8,128)(2,1)}) %all-gather.4.cloned.1.call-update) | async-done | bytes 4915216 | tf_op jit(solution)/shard_map/all_gather | solution.py:119
  104.4 4.0 %convolution_convert_fusion.1 = bf16[256,1920]{1,0:T(8,128)(2,1)S(1)} fusion(bf16[1280,1920]{1,0:T(8,128)(2,1)} %all-gather.4.cloned.1.call-done, bf16[256,1280]{1,0:T(8,128)(2,1)S(1)} %copy-done.2, f32[1280]{0:T(1024)S(1)} %copy-done.8, f32[256]{0:T(256)S(1)} %get-tuple-element.37), kind=kOutput, calls=%fused_computation.11 | convolution fusion | flops 1260093440 | bytes 6559744 | tf_op jit(solution)/shard_map/dot_general | solution.py:117
  110.5 4.7 %collective-permute-start = (bf16[64,1280]{1,0:T(8,128)(2,1)}, bf16[64,1280]{1,0:T(8,128)(2,1)}, u32[]{:S(2)}, u32[]{:S(2)}) collective-permute-start(bf16[64,1280]{1,0:T(8,128)(2,1)} %get-tuple-element.33), channel_id=1, source_target_pairs={{0,1},{1,2},{2,3},{3,4},{4,5},{5,6},{6,7},{7,8},{8,9},{9,10},{10,1... | collective-permute-start | bytes 491528 | tf_op jit(solution)/shard_map/ppermute | solution.py:19
  116.0 70.7 %all-gather.6.cloned.1.call-done = bf16[32,20,1280]{2,1,0:T(8,128)(2,1)} async-done(((bf16[1,20,1280]{2,1,0:T(8,128)(2,1)}), bf16[32,20,1280]{2,1,0:T(8,128)(2,1)}) %all-gather.6.cloned.1.call-update) | async-done | bytes 1638416 | tf_op jit(solution)/shard_map/all_gather | solution.py:129
  186.6 2.5 reshape.170
  189.1 2.0 slice.86
  191.7 1.5 reshape.156
  193.2 1.8 fusion.29
  195.9 2.5 reshape.157
  199.9 3.1 fusion.73
  203.0 1.9 fusion.19
  206.2 1.6 reshape.158
  207.8 2.0 multiply_reduce_fusion
  212.1 1.6 fusion.37
  215.2 4.3 %convolution_bitcast_fusion.1 = f32[5,64,8,80]{3,1,2,0:T(8,128)} fusion(f32[5,8,64,64]{2,3,1,0:T(8,128)} %fusion.37, bf16[5,64,8,80]{3,2,1,0:T(8,128)(2,1)S(1)} %copy-done.6, f32[5,8,64,64]{2,3,1,0:T(8,128)} %get-tuple-element.41, f32[5,8,64]{2,1,0:T(8,128)S(1)} %get-tuple-element.40), kind=kOutput, calls=%fused_computation.16 | convolution fusion | flops 27363904 | bytes 2549760 | tf_op jit(solution)/shard_map/whqk,wqhd->wkhd/dot_general | solution.py:90
  219.5 2.1 copy.44
  222.0 2.1 copy.42
  225.4 2.4 pad_maximum_fusion
  227.9 7.0 %dynamic_update_slice.3 = f32[384,1280]{1,0:T(8,128)S(1)} dynamic-update-slice(f32[384,1280]{1,0:T(8,128)S(1)} %broadcast_in_dim.20, f32[320,1280]{1,0:T(8,128)} %pad_maximum_fusion, s32[]{:T(128)S(6)} %select_n.22, s32[]{:T(128)} %constant.98.clone.1) | dynamic-update-slice | bytes 3276804 | tf_op jit(solution)/shard_map/dynamic_update_slice | solution.py:185
  237.0 3.1 collective-permute-start.2
  240.1 4.4 %convolution_bitcast_fusion.2 = bf16[5,64,8,80]{3,1,2,0:T(8,128)(2,1)} fusion(f32[5,8,64,64]{2,3,1,0:T(8,128)} %fusion.37, bf16[5,64,8,80]{3,2,1,0:T(8,128)(2,1)} %reshape.157, f32[5,8,64,64]{2,3,1,0:T(8,128)} %get-tuple-element.41, f32[5,8,64]{2,1,0:T(8,128)S(1)} %get-tuple-element.40), kind=kOutput, calls=%fused_computation.17 | convolution fusion | flops 27363904 | bytes 2140160 | tf_op jit(solution)/shard_map/whqk,wkhd->wqhd/dot_general | solution.py:89
  244.4 2.4 copy.40
  246.8 2.4 reshape.166
  251.5 1.7 fusion.50
  253.3 3.9 %collective-permute-done.3 = f32[64,1280]{1,0:T(8,128)S(1)} collective-permute-done((f32[64,1280]{1,0:T(8,128)}, f32[64,1280]{1,0:T(8,128)S(1)}, u32[]{:S(2)}, u32[]{:S(2)}) %collective-permute-start.3) | collective-permute-done | bytes 327712 | tf_op jit(solution)/shard_map/ppermute | solution.py:22
  257.2 1.8 fusion.49
  260.4 4.2 %fusion.18 = (f32[256]{0:T(256)S(1)}, f32[256,1280]{1,0:T(8,128)S(1)}) fusion(bf16[256,1280]{1,0:T(8,128)(2,1)S(1)} %copy-done.3, f32[1280]{0:T(1024)S(1)} %copy-done.8, bf16[1280,1920]{1,0:T(8,128)(2,1)} %all-gather.4.cloned.1.call-done, bf16[256,1280]{1,0:T(8,128)(2,1)S(1)} %convert.7, bf16[256,640]{1,0:T(8,128)(2,1)S(1)} %dynamic-slice_convert_fusion), kind=kOutput, calls=%fused_computation.32 | convolution fusion | flops 1261567744 | bytes 7870464 | tf_op jit(solution)/shard_map/dot_general | solution.py:193
  264.6 1.5 fusion.17
  267.4 46.7 %all_to_all.10 = bf16[16,5,5120]{2,1,0:T(8,128)(2,1)S(1)} all-to-all(bf16[16,5,5120]{2,1,0:T(8,128)(2,1)S(1)} %reshape.160), channel_id=1, replica_groups=mesh['enc'=16,'row'=32] {'enc'}, dimensions={0} | all-to-all | bytes 1638400 | tf_op jit(solution)/shard_map/all_to_all | solution.py:143
  (68 shorter events, 24.1 us)
Async XLA Ops:
  7.2 97.2 %all-gather.4.cloned.1.call-start = ((), (), s32[]{:S(2)}) async-start(), calls=%async_computation.2 | async-start | bytes 5068800 | tf_op jit(solution)/shard_map/all_gather | solution.py:119
  7.9 178.7 %all-gather.6.cloned.1.call-start = ((), (), s32[]{:S(2)}) async-start(), calls=%async_computation.3 | async-start | bytes 2027520 | tf_op jit(solution)/shard_map/all_gather | solution.py:129
  10.9 10.5 %copy-start.9 = (s32[16]{0:T(128)S(1)}, s32[16]{0:T(128)}, u32[]{:S(2)}) copy-start(s32[16]{0:T(128)} %param.18) | copy-start | bytes 196
  10.9 15.0 %copy-start.2 = (bf16[256,1280]{1,0:T(8,128)(2,1)S(1)}, bf16[256,1280]{1,0:T(8,128)(2,1)}, u32[]{:S(2)}) copy-start(bf16[256,1280]{1,0:T(8,128)(2,1)} %param.13) | copy-start | bytes 1966084
  10.9 15.2 %copy-start.10 = (s32[64]{0:T(128)S(1)}, s32[64]{0:T(128)}, u32[]{:S(2)}) copy-start(s32[64]{0:T(128)} %param.20) | copy-start | bytes 772
  10.9 15.3 %copy-start.11 = (s32[64]{0:T(128)S(1)}, s32[64]{0:T(128)}, u32[]{:S(2)}) copy-start(s32[64]{0:T(128)} %param.19) | copy-start | bytes 772
  10.9 43.8 %all-to-all-start.1 = ((bf16[16,5,5120]{2,1,0:T(8,128)(2,1)}), bf16[16,5,5120]{2,1,0:T(8,128)(2,1)S(1)}, u32[]{:S(2)}, u32[]{:S(2)}) async-start(bf16[16,5,5120]{2,1,0:T(8,128)(2,1)} %reshape.162), calls=%async_computation.1 | async-start | bytes 2621440 | tf_op jit(solution)/shard_map/all_to_all | solution.py:151
  25.9 78.4 %copy-start.8 = (f32[1280]{0:T(1024)S(1)}, f32[1280]{0:T(1024)}, u32[]{:S(2)}) copy-start(f32[1280]{0:T(1024)} %param.14) | copy-start | bytes 15364
  108.4 2.1 copy-start.5
  109.2 84.0 %collective-permute-start.1 = (bf16[64,1280]{1,0:T(8,128)(2,1)}, bf16[64,1280]{1,0:T(8,128)(2,1)}, u32[]{:S(2)}, u32[]{:S(2)}) collective-permute-start(bf16[64,1280]{1,0:T(8,128)(2,1)} %get-tuple-element.32), channel_id=1, source_target_pairs={{1,0},{2,1},{3,2},{4,3},{5,4},{6,5},{7,6},{8,7},{9,8},{10,9},{11,1... | collective-permute-start | bytes 491528 | tf_op jit(solution)/shard_map/ppermute | solution.py:22
  110.5 82.7 %collective-permute-start = (bf16[64,1280]{1,0:T(8,128)(2,1)}, bf16[64,1280]{1,0:T(8,128)(2,1)}, u32[]{:S(2)}, u32[]{:S(2)}) collective-permute-start(bf16[64,1280]{1,0:T(8,128)(2,1)} %get-tuple-element.33), channel_id=1, source_target_pairs={{0,1},{1,2},{2,3},{3,4},{4,5},{5,6},{6,7},{7,8},{8,9},{9,10},{10,1... | collective-permute-start | bytes 491528 | tf_op jit(solution)/shard_map/ppermute | solution.py:19
  189.1 2.0 slice-start
  204.9 2.9 copy-start.7
  209.8 1.1 copy-start
  210.9 1.2 copy-start.4
  212.1 1.6 copy-start.12
  213.8 1.4 copy-start.6
  237.0 14.5 %collective-permute-start.2 = (f32[64,1280]{1,0:T(8,128)}, f32[64,1280]{1,0:T(8,128)}, u32[]{:S(2)}, u32[]{:S(2)}) collective-permute-start(f32[64,1280]{1,0:T(8,128)} %get-tuple-element.29), channel_id=1, source_target_pairs={{0,1},{1,2},{2,3},{3,4},{4,5},{5,6},{6,7},{7,8},{8,9},{9,10},{10,1... | collective-permute-start | bytes 983048 | tf_op jit(solution)/shard_map/ppermute | solution.py:19
  249.2 8.0 %collective-permute-start.3 = (f32[64,1280]{1,0:T(8,128)}, f32[64,1280]{1,0:T(8,128)S(1)}, u32[]{:S(2)}, u32[]{:S(2)}) collective-permute-start(f32[64,1280]{1,0:T(8,128)} %get-tuple-element.28), channel_id=1, source_target_pairs={{1,0},{2,1},{3,2},{4,3},{5,4},{6,5},{7,6},{8,7},{9,8},{10,9},{11,1... | collective-permute-start | bytes 983048 | tf_op jit(solution)/shard_map/ppermute | solution.py:22
  253.3 7.1 %copy-start.3 = (bf16[256,1280]{1,0:T(8,128)(2,1)S(1)}, bf16[256,1280]{1,0:T(8,128)(2,1)}, u32[]{:S(2)}) copy-start(bf16[256,1280]{1,0:T(8,128)(2,1)} %param.13) | copy-start | bytes 1966084
  260.4 4.2 %copy-start.1 = (f32[256,1280]{1,0:T(8,128)S(1)}, f32[256,1280]{1,0:T(8,128)}, u32[]{:S(2)}) copy-start(f32[256,1280]{1,0:T(8,128)} %copy-done) | copy-start | bytes 3932164
Sparse Core Ops, SparseCore 0:
  11.2 93.1 all-gather.3
  107.6 79.0 all-gather.5
where the time goes:
time: 323 us; the launch traced here: 322 us
  waiting for transfers between devices  154 us (48%)
  blocking collectives  46.7 us (14%)
  local copies, waits for them, and re-layouts  41.9 us (13%)
  matrix products  28.6 us (9%)
  starting transfers between devices  20.9 us (6%)
  between operations  17.6 us (5%)
  other arithmetic  12.7 us (4%)
    all_gather x1, waiting for transfers between devices, per_device(): lax.all_gather(out_weight, 'row', axis=0, tiled=True)  70.7 us
    all_gather x1, waiting for transfers between devices, per_device(): lax.all_gather(qkv_weight, 'row', axis=0, tiled=True)  49.3 us
    all_to_all x1, blocking collectives, per_device(): lax.all_to_all(buckets.reshape(enc_devices, slot_cap, 4 * feature_width),...  46.7 us
    all_to_all x1, waiting for transfers between devices, per_device(): lax.all_to_all(llm_grads.reshape(enc_devices, slot_cap, 4 * feature_width...  28.5 us
    all_to_all x1, starting transfers between devices, per_device(): lax.all_to_all(llm_grads.reshape(enc_devices, slot_cap, 4 * feature_width...  10.5 us
    ppermute x2, starting transfers between devices, padded(): lax.ppermute(lax.slice_in_dim(block, block.shape[dim] - width, None, axis...  7.75 us
    dynamic_update_slice x1, local copies, waits for them, and re-layouts, per_device(): lax.dynamic_update_slice_in_dim(jnp.zeros((row_count + 2 * WIN, 2 * proj_...  7 us
  transfers between devices with their start and end apart: 7, of which 4 were waited for; matrix products, arithmetic and copies ran while one was open for 9% of the time, Pallas kernels for 0%

commit v1 on v0

v1 whole, which is shorter than its diff:
```python
import functools
import heapq

import jax
import jax.numpy as jnp
from jax import lax
from jax.experimental import pallas as pl
from jax.experimental.pallas import tpu as pltpu
from jax.sharding import PartitionSpec as P

HEADS = 8
HEAD_DIM = 80
WIN = 64
EPS = 1e-06

ROWS = 256
AL = ROWS + WIN
D = 1280
PROJ = HEADS * HEAD_DIM
CAP = 5
SHARD = 40
OUT_SHARD = 20
FLOWS = (512, 768)
SPLIT = 1024
SLAB = 16
SLAB_W = 1664
PIECES = ((0, 384), (384, 384), (768, 256), (1024, 256))
BLOCKS = ((0, 128, 0), (128, 128, 128), (256, 64, 192))
SLOT = 0.5

F32 = jnp.float32
BF16 = jnp.bfloat16
MESH = pl.DeviceIdType.MESH


def dot(a, b):
    return lax.dot_general(a, b, (((1,), (0,)), ((), ())), preferred_element_type=F32)


def dot_nt(a, b):
    return lax.dot_general(a, b, (((1,), (1,)), ((), ())), preferred_element_type=F32)


def dot_tn(a, b):
    return lax.dot_general(a, b, (((0,), (0,)), ((), ())), preferred_element_type=F32)


def iota(shape, dim):
    return lax.broadcasted_iota(jnp.int32, shape, dim)


def one_hot(cond):
    return jnp.where(cond, 1.0, 0.0).astype(BF16)


def ring_plan(n_x, n_z):
    dims = ((n_x, n_z), (n_z, n_x))
    tile_time = 0.16
    hop_time = 1.0

    def onward(port, da, db):
        size_a, size_b = dims[port]
        out = []
        if db == 0:
            for sign, reach in ((1, size_a // 2), (-1, size_a // 2 - 1)):
                gone = abs(da) if da * sign <= 0 else reach
                if gone < reach:
                    out.append((0, sign, reach - gone + size_b / 2))
        plus = size_b // 2 if da % 2 == 0 else size_b // 2 - 1
        for sign, reach in ((1, plus), (-1, size_b - 1 - plus)):
            gone = abs(db) if db * sign <= 0 else reach
            if gone < reach:
                out.append((1, sign, reach - gone))
        return out

    events = [[] for _ in FLOWS]
    free = {}
    waiting = {}
    count = 100
    agenda = [(0.0, f, f, (0, 0)) for f in range(len(FLOWS))]
    while agenda:
        now, _, flow, what = heapq.heappop(agenda)
        if len(what) == 2:
            port = flow
            if what != (0, 0):
                events[flow].append((now, count, "wait", what, None))
            for axis, sign, left in onward(port, *what):
                link = ("x" if axis == port else "z", sign)
                count += 2
                line = waiting.setdefault(link, [])
                heapq.heappush(line, (-left, count, flow, what, axis, sign, now))
                wake = max(now, free.get(link, 0.0))
                heapq.heappush(agenda, (wake, count + 10**6, flow, (link,)))
            continue
        link = what[0]
        if free.get(link, 0.0) > now + 1e-9 or not waiting[link]:
            continue
        _, _, flow, (da, db), axis, sign, ready = heapq.heappop(waiting[link])
        count += 2
        issue = max(ready, now - 1.0)
        hop = (sign, 0) if axis == 0 else (0, sign)
        events[flow].append((issue, count, "send", (da, db), hop))
        end = now + FLOWS[flow] / 64 * tile_time
        free[link] = end
        there = (da - sign, db) if axis == 0 else (da, db - sign)
        heapq.heappush(agenda, (end + hop_time, count, flow, there))
        heapq.heappush(agenda, (end, count + 10**6, flow, (link,)))
    return [sorted(flow_events) for flow_events in events]


def kernel(
    n_enc,
    n_x,
    n_z,
    phase_ref,
    patches_hbm,
    norm_gain_ref,
    merge_gain_ref,
    qkv_shard_ref,
    out_shard_ref,
    owner_enc_ref,
    owner_slot_ref,
    grads_hbm,
    recv2,
    pg_ref,
    patches_ref,
    grads_ref,
    wg0,
    wg1,
    w_ref,
    wo_ref,
    wo_wide,
    turn_ref,
    own_ref,
    rim_ref,
    pal_ref,
    hid_ref,
    qkv_ref,
    prob_ref,
    mask_ref,
    acc_ref,
    att_ref,
    resid_ref,
    normed_ref,
    ng_ref,
    ng_rim_ref,
    rg_ref,
    rgb_ref,
    ag_ref,
    dqkv_ref,
    dqkvb_ref,
    hg_ref,
    pal_grad_ref,
    grad_rim_ref,
    sel_ref,
    selt_ref,
    target_ref,
    slot_wide,
    slab_wide,
    send1,
    recv1,
    send2,
    relay1,
    relay2,
    w_send,
    w_recv,
    other_recv,
    slab_send,
    slab_recv,
    rim_send,
    rim_recv,
    relay_send,
    relay_recv,
    forward_send,
    own_sem,
    fetch_sem,
):
    n_row = n_x * n_z
    n_y = n_enc // 2
    n_slot = n_enc * CAP
    n_slab_rows = n_enc * SLAB
    enc = lax.axis_index("enc")
    row = lax.axis_index("row")
    core = lax.rem(enc, 2)
    y = enc // 2
    sibling = enc + 1 - 2 * core
    x = row // n_z
    z = lax.rem(row, n_z)
    left = lax.rem(row + n_row - 1, n_row)
    right = lax.rem(row + 1, n_row)
    phase = phase_ref[enc]
    edge = WIN - phase

    xs = [lax.rem(x + d, n_x) * n_z for d in range(n_x)]
    zs = [lax.rem(z + d, n_z) for d in range(n_z)]
    ys = [lax.rem(y + d, n_y) for d in range(n_y)]

    def xz(dx, dz):
        return xs[dx % n_x] + zs[dz % n_z]

    def chip(o):
        return ys[o % n_y]

    def cols(i, width):
        return pl.ds(pl.multiple_of(i * width, width), width)

    fetch_patches = pltpu.make_async_copy(patches_hbm, patches_ref, fetch_sem.at[0])
    fetch_grads = pltpu.make_async_copy(grads_hbm, grads_ref, fetch_sem.at[1])
    fetch_patches.start()
    fetch_grads.start()

    barrier = pltpu.get_barrier_semaphore()
    peers = [(enc, xz(1, 0)), (enc, xz(-1, 0)), (enc, xz(0, 1)), (enc, xz(0, -1))]
    peers += [(enc, left), (enc, right)]
    for peer in peers:
        pl.semaphore_signal(barrier, inc=1, device_id=peer, device_id_type=MESH)

    @pl.loop(1, n_enc)
    def _(d):
        pl.semaphore_signal(
            barrier, inc=1, device_id=(lax.rem(enc + d, n_enc), row), device_id_type=MESH
        )

    q_wide = qkv_shard_ref[...].astype(F32)
    odd_z = lax.rem(z, 2)
    odd = odd_z
    m = iota((SHARD, 1), 0)
    from_left = jnp.where(m < 16, m + 4 * odd, -1)
    from_left = jnp.where((m >= 32) & (m < 36), m - 16 - 64 * odd, from_left)
    from_left = jnp.where(m >= 36, m - 36 - 64 * (1 - odd), from_left)
    from_right = jnp.where((m >= 16) & (m < 32), m - 16 + 4 * odd, -1)
    from_right = jnp.where((m >= 32) & (m < 36), m - 32 - 64 * (1 - odd), from_right)
    from_right = jnp.where(m >= 36, m - 20 - 64 * odd, from_right)
    source = iota((SHARD, OUT_SHARD), 1)
    out40 = dot(one_hot(source == from_left), out_shard_ref[:, :PROJ]) + dot(
        one_hot(source == from_right), out_shard_ref[:, PROJ:]
    )

    def stacked(*parts):
        return jnp.concatenate(parts, 0).astype(BF16)

    wg0[row] = stacked(q_wide[:, :512], q_wide[:, 512:SPLIT])
    wg1[row] = stacked(q_wide[:, SPLIT:1792], jnp.concatenate([q_wide[:, 1792:], out40], 1))

    pl.semaphore_wait(barrier, len(peers) + n_enc - 1)

    plans = ring_plan(n_x, n_z)
    bufs = (wg0, wg1)

    def place(port, da, db):
        return xz(da, db) if port == 0 else xz(db, da)

    def block_wait(port, block):
        buf, r = bufs[port], place(port, *block)
        pltpu.make_async_copy(buf.at[r], buf.at[r], w_recv.at[r]).wait()

    def block_send(port, block, hop):
        buf, r = bufs[port], place(port, *block)
        pltpu.make_async_remote_copy(
            src_ref=buf.at[r],
            dst_ref=buf.at[r],
            send_sem=w_send.at[0],
            recv_sem=w_recv.at[r],
            device_id=(enc, place(port, *hop)),
            device_id_type=MESH,
        ).start()

    def hand_over(ref, send_sem, recv_sem):
        pltpu.make_async_remote_copy(
            src_ref=ref,
            dst_ref=ref,
            send_sem=send_sem,
            recv_sem=recv_sem,
            device_id=(sibling, row),
            device_id_type=MESH,
        ).start()

    def pack_pair(port, j):
        rows = pl.ds(pl.multiple_of(j * 2 * SHARD, 2 * SHARD), 2 * SHARD)
        out_rows = pl.ds(pl.multiple_of(j * 2 * OUT_SHARD, 8), 2 * OUT_SHARD)

        def halves(top):
            return [bufs[port][2 * j + k, top : top + SHARD, :].astype(F32) for k in range(2)]

        if port == 0:
            w_ref[rows, :512] = stacked(*halves(0))
            w_ref[rows, 512:SPLIT] = stacked(*halves(SHARD))
            hand_over(w_ref.at[rows, pl.ds(0, SPLIT)], w_send.at[1], other_recv.at[0])
            return
        w_ref[rows, SPLIT:1792] = stacked(*halves(0))
        even, odd = halves(SHARD)
        w_ref[rows, 1792:] = stacked(even[:, :128], odd[:, :128])
        hand_over(w_ref.at[rows, pl.ds(SPLIT, 3 * PROJ - SPLIT)], w_send.at[1], other_recv.at[0])
        even, odd = even[:, 128:], odd[:, 128:]
        upper = iota((8, 1), 0) < 4
        middle = jnp.where(upper, even[32:], odd[32:])
        wo_wide[out_rows, :PROJ] = jnp.concatenate([even[:16], middle, odd[:16]], 0)
        middle = pltpu.roll(jnp.where(upper, odd[32:], even[32:]), 4, 0)
        wo_wide[out_rows, PROJ:] = jnp.concatenate([even[16:32], middle, odd[16:32]], 0)
        hand_over(wo_wide.at[out_rows], w_send.at[2], other_recv.at[1])

    def rows_wait(ref, sem):
        pltpu.make_async_copy(ref, ref, sem).wait()

    def port_rows(port):
        return w_ref.at[:, pl.ds(0, SPLIT) if port == 0 else pl.ds(SPLIT, 3 * PROJ - SPLIT)]

    def slot_of(event):
        return int(event[0] / SLOT)

    n_slots = max(slot_of(plan[-1]) for plan in plans) + 1

    def pairs_after(port):
        arrival = {(0, 0): 0}
        for event in plans[port]:
            if event[2] == "wait":
                da, db = event[3]
                dx, dz = (da, db) if port == 0 else (db, da)
                arrival[dx % n_x, dz % n_z] = slot_of(event)
        found = []
        for m in range(1, n_z // 2 + 1):
            even, odd = (m - 1, -m) if m % 2 else (-m, m - 1)
            for dx in range(n_x):
                last = max(
                    arrival[dx, (start + k) % n_z] for start in (even, odd) for k in range(2)
                )
                found.append((last, dx, even, odd))
        return found

    def run_slot(port, slot):
        for event in plans[port]:
            if slot_of(event) == slot:
                _, _, kind, block, hop = event
                if kind == "wait":
                    block_wait(port, block)
                else:
                    block_send(port, block, hop)
        for last, dx, even, odd in pairs_after(port):
            if last == slot:
                first = xz(dx, even) + (xz(dx, odd) - xz(dx, even)) * odd_z
                pack_pair(port, first // 2)

    def weights_slot(slot):
        for port in range(2):
            if any(slot_of(event) == slot for event in plans[port]):

                @pl.when(core == port)
                def _():
                    run_slot(port, slot)

    def weights_wait():
        for port in range(2):

            @pl.when(core != port)
            def _():
                rows_wait(port_rows(port), other_recv.at[0])
                if port == 1:
                    rows_wait(wo_wide, other_recv.at[1])

    def weights_drain():
        blocks = pl.ds(0, n_row - 1)
        for port in range(2):

            @pl.when(core == port)
            def _():
                rows_wait(bufs[port].at[blocks], w_send.at[0])
                rows_wait(port_rows(port), w_send.at[1])
                if port == 1:
                    rows_wait(wo_wide, w_send.at[2])

    def rim_copy(index, src, dst, target):
        return pltpu.make_async_remote_copy(
            src_ref=src,
            dst_ref=dst,
            send_sem=rim_send.at[index],
            recv_sem=rim_recv.at[index],
            device_id=(enc, target),
            device_id_type=MESH,
        )

    top = pl.ds(0, WIN)
    rims = (
        rim_copy(0, own_ref.at[top], rim_ref.at[0], right),
        rim_copy(1, own_ref.at[top], rim_ref.at[1], left),
    )
    ng_rim = rim_copy(2, ng_ref.at[top], ng_rim_ref, right)
    grad_rim = rim_copy(3, pal_grad_ref.at[top], grad_rim_ref, left)

    def slab(ref, e):
        return ref.at[pl.ds(pl.multiple_of(SLAB * e, SLAB), SLAB)]

    def exchange_copy(index, send, recv, peer):
        return pltpu.make_async_remote_copy(
            src_ref=slab(send, peer),
            dst_ref=slab(recv, enc),
            send_sem=slab_send.at[index],
            recv_sem=slab_recv.at[index],
            device_id=(peer, row),
            device_id_type=MESH,
        )

    def near_peers():
        for o in range(n_y // 2 - 1, 0, -1):
            ahead, behind = chip(o), chip(-o)
            for side in (0, 1):
                turned = ahead + (behind - ahead) * (core if side == 0 else 1 - core)
                for k in range(2):
                    yield 2 * turned + k
        yield sibling

    next_chip = chip(1) + (chip(-1) - chip(1)) * core
    last_chip = chip(-1) + (chip(1) - chip(-1)) * core
    far_chip = chip(n_y // 2 - 1) + (chip(n_y // 2 + 1) - chip(n_y // 2 - 1)) * core

    def relay_copy(index, send):
        pair = pl.ds(pl.multiple_of(2 * SLAB * chip(n_y // 2), 2 * SLAB), 2 * SLAB)
        return pltpu.make_async_remote_copy(
            src_ref=send.at[pair],
            dst_ref=(relay1, relay2)[index],
            send_sem=relay_send.at[index],
            recv_sem=relay_recv.at[index],
            device_id=(2 * next_chip + core, row),
            device_id_type=MESH,
        )

    def forward_copy(index, recv, k):
        origin = 2 * last_chip + core
        return pltpu.make_async_remote_copy(
            src_ref=(relay1, relay2)[index].at[pl.ds(SLAB * k, SLAB)],
            dst_ref=slab(recv, origin),
            send_sem=forward_send.at[index],
            recv_sem=slab_recv.at[index],
            device_id=(2 * far_chip + k, row),
            device_id_type=MESH,
        )

    def own_copy(index, send, recv):
        return pltpu.make_async_copy(slab(send, enc), slab(recv, enc), own_sem.at[index])

    def exchange_start(index, send, recv):
        relay_copy(index, send).start()
        for peer in near_peers():
            exchange_copy(index, send, recv, peer).start()
        own_copy(index, send, recv).start()

    def exchange_forward(index, recv):
        relay_copy(index, send1).wait_recv()
        for k in range(2):
            forward_copy(index, recv, k).start()

    def exchange_wait(index, send, recv):
        own_copy(index, send, recv).wait()
        rows_wait(recv.at[pl.ds(0, (n_enc - 1) * SLAB)], slab_recv.at[index])

    def exchange_drain(index, send):
        relay_copy(index, send).wait_send()
        rows_wait(send.at[pl.ds(0, (n_enc - 3) * SLAB)], slab_send.at[index])
        rows_wait((relay1, relay2)[index], forward_send.at[index])

    def rotate():
        fetch_patches.wait()
        turn = iota((ROWS, ROWS), 1) == ((iota((ROWS, ROWS), 0) - edge) & (ROWS - 1))
        turn_ref[...] = one_hot(turn)
        for c in range(0, D, 256):
            part = dot(turn_ref[...], patches_ref[:, c : c + 256])
            own_ref[:, c : c + 256] = part.astype(BF16)
        for copy in rims:
            copy.start()

    n_tile = D // 128

    def grads_wide(q0, q1):
        if q0 == 0:
            fetch_grads.wait()
        for t in range(q0 * n_tile, q1 * n_tile):
            slot_wide[t] = grads_ref[:, 128 * t : 128 * t + 128].astype(F32)

    def grads_move(q):
        for t in range(n_tile):
            at = q * n_tile + t
            for slot in range(4):
                part = slot_wide[at, pl.ds(slot, n_enc, stride=CAP), :]
                slab_wide[t, pl.ds(4 * slot + q, n_enc, stride=SLAB), :] = part
        for p, (off, width) in enumerate(PIECES):
            for t in range(3):
                if t < width // 128:
                    at = (q * D + off) // 128 + t
                    part = slot_wide[at, pl.ds(4, n_enc, stride=CAP), :]
                else:
                    part = jnp.zeros((n_enc, 128), F32)
                slab_wide[n_tile + t, pl.ds(4 * q + p, n_enc, stride=SLAB), :] = part

    def grads_pack(first, last):
        for t in range(first, last):
            send1[:, 128 * t : 128 * t + 128] = slab_wide[t].astype(BF16)
        if last == SLAB_W // 128:
            exchange_start(0, send1, recv1)

    n_tok = ROWS // 4

    def targets(code, patch):
        slot, base = code & 7, (code >> 3) * 16
        quarter = patch & 3
        target_a = jnp.where(slot < 4, base + slot * 4 + quarter, -1)
        target_b = jnp.where(slot == 4, base + quarter * 4, -8)
        return target_a, target_b

    def selector_targets():
        code_row = owner_enc_ref[...] * 8 + owner_slot_ref[...]
        square = iota((n_tok, n_tok), 0) == iota((n_tok, n_tok), 1)
        code_col = jnp.sum(jnp.where(square, code_row, 0), 1, keepdims=True)
        patch = (iota((1, ROWS), 1) - edge) & (ROWS - 1)
        tok = iota((n_tok, ROWS), 0) == (patch >> 2)
        code = jnp.sum(jnp.where(tok, code_col, 0), 0, keepdims=True)
        target_ref[0:1, :], target_ref[1:2, :] = targets(code, patch)

    def selector(p):
        bucket = iota((n_slab_rows, ROWS), 0)
        target = target_ref[0:1, :] if p == 0 else target_ref[1:2, :] + (p - 1)
        sel_ref[p] = one_hot(bucket == target)

    def selectors_back():
        code_row = owner_enc_ref[...] * 8 + owner_slot_ref[...]
        patch = (iota((ROWS, 1), 0) - edge) & (ROWS - 1)
        tok = iota((ROWS, n_tok), 1) == (patch >> 2)
        code = jnp.sum(jnp.where(tok, code_row, 0), 1, keepdims=True)
        target_a, target_b = targets(code, patch)
        bucket = iota((ROWS, n_slab_rows), 1)
        selt_ref[0] = one_hot(bucket == target_a)
        for p in range(4):
            selt_ref[1 + p] = one_hot(bucket == target_b + p)

    def piece(body, *args):
        return lambda: body(*args)

    def masks(r0, count, k0):
        i = iota((count, 128), 0) + r0
        j = iota((count, 128), 1) + k0
        first = jnp.where(row == 0, 0, -1)
        last = jnp.where(row == n_row - 1, ROWS // WIN, -1)
        ends = ((i >> 6) == first) | ((i >> 6) == last)
        i_low = jnp.where((i & (WIN - 1)) < edge, 1, 0)
        j_low = jnp.where((j & (WIN - 1)) < edge, 1, 0)
        apart = jnp.where(ends, i_low ^ j_low, 0)
        same = ((i >> 6) == (j >> 6)) & (apart == 0)
        mask_ref[r0 : r0 + count, :] = jnp.where(same, 1.0, 0.0)

    def zeros():
        acc_ref[...] = jnp.zeros_like(acc_ref)

    below = iota((WIN, 1), 0) < edge

    def rims_in():
        for copy in rims:
            copy.wait()
        pal_ref[:WIN, :] = jnp.where(below, rim_ref[0], own_ref[:WIN, :])
        pal_ref[WIN:ROWS, :] = own_ref[WIN:, :]
        pal_ref[ROWS:, :] = jnp.where(below, own_ref[:WIN, :], rim_ref[1])

    def rms_norm(src, dst, gain_ref, rows):
        wide = src[rows, :].astype(F32)
        inv = lax.rsqrt(jnp.mean(wide * wide, -1, keepdims=True) + EPS)
        dst[rows, :] = (wide * inv * gain_ref[...].reshape(1, D)).astype(BF16)

    def rms_back(wide, gain_ref, upstream_in):
        inv = lax.rsqrt(jnp.mean(wide * wide, -1, keepdims=True) + EPS)
        upstream = upstream_in * gain_ref[...].reshape(1, D)
        inner = jnp.mean(upstream * wide, -1, keepdims=True)
        return inv * upstream - wide * (inv * inv * inv) * inner

    def piece(body, *args):
        return lambda: body(*args)

    def project(c0, c1):
        for c in range(c0, c1, 256):
            w = min(256, c1 - c)
            part = dot(hid_ref[...], w_ref[:, c : c + w])
            qkv_ref[:, c : c + w] = part.astype(BF16)

    scale = HEAD_DIM ** (-0.5)
    pairs = range(HEADS // 2)

    def window(t, base=0):
        return slice(base + 128 * t, base + 128 * t + 256)

    def two_heads(t, value):
        lane = iota((1, 256), 1) - 32 * t
        zero = jnp.zeros_like(value)
        first = jnp.where((lane >= 0) & (lane < HEAD_DIM), value, zero)
        second = jnp.where((lane >= HEAD_DIM) & (lane < 2 * HEAD_DIM), value, zero)
        return jnp.concatenate([first, second], 0)

    def attend(t):
        for r0, count, k0 in BLOCKS:
            rows, keys = slice(r0, r0 + count), slice(k0, k0 + 128)
            scores = dot_nt(qkv_ref[rows, window(t)], two_heads(t, qkv_ref[keys, window(t, PROJ)]))
            seen = mask_ref[rows, :] > 0.5
            both = []
            for g in range(2):
                s = jnp.where(seen, scores[:, 128 * g : 128 * g + 128] * scale, -1e30)
                e = jnp.exp(s - jnp.max(s, -1, keepdims=True))
                p = e / jnp.sum(e, -1, keepdims=True)
                if r0 < ROWS:
                    prob_ref[2 * t + g, rows, :] = p
                both.append(p.astype(BF16))
            values = two_heads(t, qkv_ref[keys, window(t, 2 * PROJ)])
            acc_ref[rows, window(t)] += dot(jnp.concatenate(both, 1), values)

    work = [piece(grads_wide, 0, 2), piece(grads_wide, 2, 4)]
    work += [piece(grads_move, q) for q in range(4)]
    work += [piece(grads_pack, 0, SLAB_W // 128)]
    work += [piece(masks, *block) for block in BLOCKS]
    work += [rims_in, selector_targets]
    for k in range(5):
        rows = slice(k * WIN, (k + 1) * WIN)
        work += [piece(selector, k), piece(rms_norm, pal_ref, hid_ref, norm_gain_ref, rows)]
    work += [zeros]
    for slot in range(n_slots):
        weights_slot(slot)
        if slot == 0:
            rotate()
        elif work:
            work.pop(0)()
        if slot == 20:
            exchange_forward(0, recv1)
    assert not work
    weights_wait()
    project(0, 3 * PROJ)
    for t in pairs:
        attend(t)

    att_ref[...] = acc_ref[...].astype(BF16)

    @pl.loop(0, D // 256)
    def _(i):
        c = cols(i, 256)
        wo_ref[:, c] = wo_wide[:, c].astype(BF16)
        branch = dot(att_ref[...], wo_ref[:, c])
        resid_ref[:, c] = (pal_ref[:, c].astype(F32) + branch).astype(BF16)

    @pl.loop(0, AL // WIN)
    def _(i):
        rows = pl.ds(pl.multiple_of(i * WIN, WIN), WIN)
        rms_norm(resid_ref, normed_ref, merge_gain_ref, rows)

    normed_ref[:WIN, :] = jnp.where(below, normed_ref[ROWS:, :], normed_ref[:WIN, :])

    for c in range(0, D, 256):
        send2[:, c : c + 256] = dot(sel_ref[0], normed_ref[:ROWS, c : c + 256]).astype(BF16)
    head_part = jnp.zeros((n_slab_rows, 256), F32)
    tail_part = jnp.zeros((n_slab_rows, 128), F32)
    for p, (off, width) in enumerate(PIECES):
        head_part += dot(sel_ref[1 + p], normed_ref[:ROWS, off : off + 256])
        if width > 256:
            tail_part += dot(sel_ref[1 + p], normed_ref[:ROWS, off + 256 : off + width])
    send2[:, D : D + 256] = head_part.astype(BF16)
    send2[:, D + 256 :] = tail_part.astype(BF16)
    exchange_start(1, send2, recv2)

    selectors_back()
    dqkv_ref[...] = jnp.zeros_like(dqkv_ref)
    exchange_wait(0, send1, recv1)

    def gradients(rows):
        for p, (off, width) in enumerate(PIECES):
            for c in range(0, width, 256):
                w = min(256, width - c)
                part = dot(selt_ref[0, rows], recv1[:, off + c : off + c + w])
                part += dot(selt_ref[1 + p, rows], recv1[:, D + c : D + c + w])
                ng_ref[rows, off + c : off + c + w] = part.astype(BF16)

    gradients(slice(0, WIN))
    ng_rim.start()
    gradients(slice(WIN, ROWS))

    def merge_back(rows, grad_in):
        grad = rms_back(resid_ref[rows, :].astype(F32), merge_gain_ref, grad_in.astype(F32))
        rg_ref[rows, :] = grad
        rgb_ref[rows, :] = grad.astype(BF16)

    @pl.loop(1, ROWS // WIN)
    def _(i):
        rows = pl.ds(pl.multiple_of(i * WIN, WIN), WIN)
        merge_back(rows, ng_ref[rows, :])

    ng_rim.wait()
    merge_back(slice(0, WIN), jnp.where(below, ng_rim_ref[...], ng_ref[:WIN, :]))

    exchange_forward(1, recv2)

    for c0, c1 in ((0, 256), (256, 512), (512, 640)):
        ag_ref[:, c0:c1] = dot_nt(rgb_ref[...], wo_ref[c0:c1, :]).astype(BF16)

    for t in pairs:
        for r0 in (0, 128):
            rows = slice(r0, r0 + 128)
            grad = ag_ref[rows, window(t)]
            values = two_heads(t, qkv_ref[rows, window(t, 2 * PROJ)])
            keys = two_heads(t, qkv_ref[rows, window(t, PROJ)])
            dp = dot_nt(grad, values)
            probs, score_grads = [], []
            for g in range(2):
                p = prob_ref[2 * t + g, rows, :]
                dp_g = dp[:, 128 * g : 128 * g + 128]
                centred = dp_g - jnp.sum(p * dp_g, -1, keepdims=True)
                score_grads.append((p * centred * scale).astype(BF16))
                probs.append(p.astype(BF16))
            dq = dot(jnp.concatenate(score_grads, 1), keys)
            queries = two_heads(t, qkv_ref[rows, window(t)])
            dk = dot_tn(jnp.concatenate(score_grads, 0), queries)
            dv = dot_tn(jnp.concatenate(probs, 0), two_heads(t, grad))
            dqkv_ref[rows, window(t)] += dq
            dqkv_ref[rows, window(t, PROJ)] += dk
            dqkv_ref[rows, window(t, 2 * PROJ)] += dv

    dqkvb_ref[...] = dqkv_ref[...].astype(BF16)

    @pl.loop(0, D // 256)
    def _(i):
        c = cols(i, 256)
        hg_ref[:, c] = dot_nt(dqkvb_ref[...], w_ref[c, :])

    def norm_back(rows):
        grad = rms_back(pal_ref[rows, :].astype(F32), norm_gain_ref, hg_ref[rows, :])
        pal_grad_ref[rows, :] = (rg_ref[rows, :] + grad).astype(BF16)

    norm_back(slice(0, WIN))
    grad_rim.start()

    @pl.loop(1, ROWS // WIN)
    def _(i):
        norm_back(pl.ds(pl.multiple_of(i * WIN, WIN), WIN))

    grad_rim.wait()
    own_ref[:WIN, :] = jnp.where(below, grad_rim_ref[...], pal_grad_ref[:WIN, :])
    own_ref[WIN:, :] = pal_grad_ref[WIN:, :]
    for c in range(0, D, 256):
        part = dot_tn(turn_ref[...], own_ref[:, c : c + 256])
        pg_ref[:, c : c + 256] = part.astype(BF16)

    exchange_drain(0, send1)
    weights_drain()
    exchange_drain(1, send2)
    exchange_wait(1, send2, recv2)


def place_kernel(n_enc, slabs_ref, grads_ref, llm_ref, pg_ref, wide_ref, llm_wide):
    for t in range(SLAB_W // 128):
        wide_ref[t] = slabs_ref[:, 128 * t : 128 * t + 128].astype(F32)
    for q in range(4):
        for t in range(D // 128):
            at = q * (D // 128) + t
            for slot in range(4):
                part = wide_ref[t, pl.ds(4 * slot + q, n_enc, stride=SLAB), :]
                llm_wide[at, pl.ds(slot, n_enc, stride=CAP), :] = part
        for p, (off, width) in enumerate(PIECES):
            for t in range(width // 128):
                at = (q * D + off) // 128 + t
                part = wide_ref[D // 128 + t, pl.ds(4 * q + p, n_enc, stride=SLAB), :]
                llm_wide[at, pl.ds(4, n_enc, stride=CAP), :] = part
    for t in range(4 * D // 128):
        llm_ref[:, 128 * t : 128 * t + 128] = llm_wide[t].astype(BF16)
    pg_ref[...] = grads_ref[...]


def per_device(
    n_enc,
    n_x,
    n_z,
    patches,
    norm_gain,
    merge_gain,
    qkv_weight,
    out_weight,
    window_phase,
    owner_enc,
    owner_slot,
    llm_grads,
):
    n_row = n_x * n_z
    n_slot = n_enc * CAP
    vmem = pl.BlockSpec(memory_space=pltpu.VMEM)
    smem = pl.BlockSpec(memory_space=pltpu.SMEM)
    anywhere = pl.BlockSpec(memory_space=pl.ANY)
    dma = pltpu.SemaphoreType.DMA
    slabs = pltpu.VMEM((n_enc * SLAB, SLAB_W), BF16)
    slabs_in, grads_in = pl.pallas_call(
        functools.partial(kernel, n_enc, n_x, n_z),
        out_shape=(
            jax.ShapeDtypeStruct((n_enc * SLAB, SLAB_W), BF16),
            jax.ShapeDtypeStruct((ROWS, D), BF16),
        ),
        in_specs=[smem, anywhere] + [vmem] * 6 + [anywhere],
        out_specs=(anywhere, vmem),
        scratch_shapes=[
            pltpu.VMEM((ROWS, D), BF16),
            pltpu.VMEM((n_slot, 4 * D), BF16),
            *(pltpu.VMEM((n_row, 2 * SHARD, width), BF16) for width in FLOWS),
            pltpu.VMEM((D, 3 * PROJ), BF16),
            pltpu.VMEM((PROJ, D), BF16),
            pltpu.VMEM((PROJ, D), F32),
            pltpu.VMEM((ROWS, ROWS), BF16),
            pltpu.VMEM((ROWS, D), BF16),
            pltpu.VMEM((2, WIN, D), BF16),
            pltpu.VMEM((AL, D), BF16),
            pltpu.VMEM((AL, D), BF16),
            pltpu.VMEM((AL, 3 * PROJ), BF16),
            pltpu.VMEM((HEADS, ROWS, 128), F32),
            pltpu.VMEM((AL, 128), F32),
            pltpu.VMEM((AL, PROJ), F32),
            pltpu.VMEM((AL, PROJ), BF16),
            pltpu.VMEM((AL, D), BF16),
            pltpu.VMEM((AL, D), BF16),
            pltpu.VMEM((ROWS, D), BF16),
            pltpu.VMEM((WIN, D), BF16),
            pltpu.VMEM((ROWS, D), F32),
            pltpu.VMEM((ROWS, D), BF16),
            pltpu.VMEM((ROWS, PROJ), BF16),
            pltpu.VMEM((ROWS, 3 * PROJ), F32),
            pltpu.VMEM((ROWS, 3 * PROJ), BF16),
            pltpu.VMEM((ROWS, D), F32),
            pltpu.VMEM((ROWS, D), BF16),
            pltpu.VMEM((WIN, D), BF16),
            pltpu.VMEM((5, n_enc * SLAB, ROWS), BF16),
            pltpu.VMEM((5, ROWS, n_enc * SLAB), BF16),
            pltpu.VMEM((8, ROWS), jnp.int32),
            pltpu.VMEM((4 * D // 128, n_slot, 128), F32),
            pltpu.VMEM((SLAB_W // 128, n_enc * SLAB, 128), F32),
            slabs,
            slabs,
            slabs,
            pltpu.VMEM((2 * SLAB, SLAB_W), BF16),
            pltpu.VMEM((2 * SLAB, SLAB_W), BF16),
            dma((3,)),
            dma((n_row,)),
            dma((2,)),
            dma((2,)),
            dma((2,)),
            dma((4,)),
            dma((4,)),
            dma((2,)),
            dma((2,)),
            dma((2,)),
            dma((2,)),
            dma((2,)),
        ],
        compiler_params=pltpu.CompilerParams(
            collective_id=0, has_side_effects=True, vmem_limit_bytes=56 * 1024 * 1024
        ),
        cost_estimate=pl.CostEstimate(flops=8_000_000_000, bytes_accessed=4_000_000, transcendentals=400000),
    )(
        window_phase,
        patches,
        norm_gain,
        merge_gain,
        qkv_weight,
        out_weight,
        owner_enc.reshape(1, -1),
        owner_slot.reshape(1, -1),
        llm_grads,
    )
    return pl.pallas_call(
        functools.partial(place_kernel, n_enc),
        out_shape=(
            jax.ShapeDtypeStruct((n_slot, 4 * D), BF16),
            jax.ShapeDtypeStruct((ROWS, D), BF16),
        ),
        in_specs=[vmem, vmem],
        out_specs=(vmem, vmem),
        scratch_shapes=[
            pltpu.VMEM((SLAB_W // 128, n_enc * SLAB, 128), F32),
            pltpu.VMEM((4 * D // 128, n_slot, 128), F32),
        ],
        compiler_params=pltpu.CompilerParams(vmem_limit_bytes=60 * 1024 * 1024),
        cost_estimate=pl.CostEstimate(
            flops=1_000_000, bytes_accessed=3_200_000, transcendentals=0
        ),
    )(slabs_in, grads_in)


def solution(mesh):
    n_enc, n_row = mesh.shape["enc"], mesh.shape["row"]
    n_x = 4
    in_specs = (
        P(("enc", "row"), None),
        P(),
        P(),
        P("row", None),
        P("row", None),
        P(),
        P(("enc", "row")),
        P(("enc", "row")),
        P(("enc", "row"), None),
    )
    out_specs = (P(("enc", "row"), None), P(("enc", "row"), None))
    return jax.shard_map(
        functools.partial(per_device, n_enc, n_x, n_row // n_x),
        mesh=mesh,
        in_specs=in_specs,
        out_specs=out_specs,
        check_vma=False,
    )
```

time: 323 us -> 84.3 us (0.26)
  waiting for transfers between devices: 154 us -> 0 us
  Pallas kernels: 0 us -> 83.5 us
  blocking collectives: 46.7 us -> 0 us
  local copies, waits for them, and re-layouts: 41.9 us -> 0 us
  matrix products: 28.6 us -> 0 us
  starting transfers between devices: 20.9 us -> 0 us
  between operations: 17.6 us -> 0.64 us
  other arithmetic: 12.7 us -> 0 us
    all_gather x2 -> x0, waiting for transfers between devices: 120 us -> none  [the longest x1 70.7 us: per_device(): lax.all_gather(out_weight, 'row', axis=0, tiled=True)]
    pallas_call x0 -> x2, Pallas kernels: none -> 83.5 us  [the longest x1 80.3 us: per_device(): pl.pallas_call(functools.partial(kernel, n_enc, n_x, n_z), out_shape=(jax...]
    all_to_all x1 -> x0, blocking collectives: 46.7 us -> none  [per_device(): lax.all_to_all(buckets.reshape(enc_devices, slot_cap, 4 * feature_width),...]
    all_to_all x1 -> x0, waiting for transfers between devices: 28.5 us -> none  [per_device(): lax.all_to_all(llm_grads.reshape(enc_devices, slot_cap, 4 * feature_width...]
    dot_general x11 -> x0, matrix products: 25.5 us -> none  [the longest x1 4.37 us: window_backward(): jnp.einsum('whqk,wkhd->wqhd', score_grad, k_four, preferred_element_type=...]
    reshape x14 -> x0, local copies, waits for them, and re-layouts: 16.8 us -> none  [the longest x3 4.06 us: window_backward(): return (dq_four.reshape(flat), dk_four.reshape(flat), dv_four.reshape(flat))]
    all_to_all x1 -> x0, starting transfers between devices: 10.5 us -> none  [per_device(): lax.all_to_all(llm_grads.reshape(enc_devices, slot_cap, 4 * feature_width...]
    ppermute x4 -> x0, starting transfers between devices: 10.3 us -> none  [the longest x2 7.75 us: padded(): lax.ppermute(lax.slice_in_dim(block, block.shape[dim] - width, None, axis...]
  transfers between devices with their start and end apart: 7 -> 0, of which waited for: 4 -> 0; matrix products, arithmetic and copies ran while one was open for 9% -> 0% of each run, Pallas kernels for 0% -> 0%
where the time goes in v1:
time: 84.3 us; the launch traced here: 84.2 us
  Pallas kernels  83.5 us (99%)
    pallas_call x1, Pallas kernels, per_device(): pl.pallas_call(functools.partial(kernel, n_enc, n_x, n_z), out_shape=(jax...  80.3 us
    pallas_call x1, Pallas kernels, per_device(): pl.pallas_call(functools.partial(place_kernel, n_enc), out_shape=(jax.Sha...  3.23 us

profile of v1, /device:TPU:1, one launch (start us, length us, event | category | flops | bytes accessed | tf_op | source)
XLA Modules:
  0.0 84.2 jit_solution(8373258790962978835)
XLA Ops:
  0.6 80.3 %shard_map.104 = (bf16[256,1664]{1,0:T(8,128)(2,1)}, bf16[256,1280]{1,0:T(8,128)(2,1)}) custom-call(s32[16]{0:T(128)} %phase_ref.1, bf16[256,1280]{1,0:T(8,128)(2,1)} %patches_hbm.1, f32[1280]{0:T(1024)} %norm_gain_ref.1, f32[1280]{0:T(1024)} %merge_gain_ref.1, bf16[40,1920]{1,0:T(8,128)(2,1)} %qkv_shard_ref.1, bf16[20,1280]{1,0:T(8,128)(2,1)} %out_shard_ref.1, ...), custom_call_target="tpu_custom_call" | custom-call | flops 8000000000 | bytes 4000000 | tf_op jit(solution)/shard_map/pallas_call | solution.py:787
  80.9 3.2 %shard_map.105 = (bf16[80,5120]{1,0:T(8,128)(2,1)}, bf16[256,1280]{1,0:T(8,128)(2,1)}) custom-call(bf16[256,1664]{1,0:T(8,128)(2,1)} %get-tuple-element.4.slabs_ref, bf16[256,1280]{1,0:T(8,128)(2,1)} %get-tuple-element.5.grads_ref), custom_call_target="tpu_custom_call" | custom-call | flops 1000000 | bytes 3200000 | tf_op jit(solution)/shard_map/pallas_call | solution.py:862

commit v2 on v1

--- a/solution.py
+++ b/solution.py
@@ -138,7 +138,6 @@
     qkv_ref,
     prob_ref,
     mask_ref,
-    acc_ref,
     att_ref,
     resid_ref,
     normed_ref,
@@ -147,7 +146,6 @@
     rg_ref,
     rgb_ref,
     ag_ref,
-    dqkv_ref,
     dqkvb_ref,
     hg_ref,
     pal_grad_ref,
@@ -348,15 +346,6 @@
                 def _():
                     run_slot(port, slot)
 
-    def weights_wait():
-        for port in range(2):
-
-            @pl.when(core != port)
-            def _():
-                rows_wait(port_rows(port), other_recv.at[0])
-                if port == 1:
-                    rows_wait(wo_wide, other_recv.at[1])
-
     def weights_drain():
         blocks = pl.ds(0, n_row - 1)
         for port in range(2):
@@ -545,9 +534,6 @@
         same = ((i >> 6) == (j >> 6)) & (apart == 0)
         mask_ref[r0 : r0 + count, :] = jnp.where(same, 1.0, 0.0)
 
-    def zeros():
-        acc_ref[...] = jnp.zeros_like(acc_ref)
-
     below = iota((WIN, 1), 0) < edge
 
     def rims_in():
@@ -590,9 +576,18 @@
         second = jnp.where((lane >= HEAD_DIM) & (lane < 2 * HEAD_DIM), value, zero)
         return jnp.concatenate([first, second], 0)
 
-    def attend(t):
-        for r0, count, k0 in BLOCKS:
-            rows, keys = slice(r0, r0 + count), slice(k0, k0 + 128)
+    def join(ref, rows, base, t, value, carry):
+        low = value[:, :128] if carry is None else value[:, :128] + carry
+        ref[rows, base + 128 * t : base + 128 * t + 128] = low.astype(BF16)
+        high = value[:, 128:]
+        if t == pairs[-1]:
+            ref[rows, base + 128 * t + 128 : base + 128 * t + 256] = high.astype(BF16)
+        return high
+
+    def attend(r0, count, k0):
+        rows, keys = slice(r0, r0 + count), slice(k0, k0 + 128)
+        carry = None
+        for t in pairs:
             scores = dot_nt(qkv_ref[rows, window(t)], two_heads(t, qkv_ref[keys, window(t, PROJ)]))
             seen = mask_ref[rows, :] > 0.5
             both = []
@@ -604,7 +599,7 @@
                     prob_ref[2 * t + g, rows, :] = p
                 both.append(p.astype(BF16))
             values = two_heads(t, qkv_ref[keys, window(t, 2 * PROJ)])
-            acc_ref[rows, window(t)] += dot(jnp.concatenate(both, 1), values)
+            carry = join(att_ref, rows, 0, t, dot(jnp.concatenate(both, 1), values), carry)
 
     work = [piece(grads_wide, 0, 2), piece(grads_wide, 2, 4)]
     work += [piece(grads_move, q) for q in range(4)]
@@ -614,7 +609,7 @@
     for k in range(5):
         rows = slice(k * WIN, (k + 1) * WIN)
         work += [piece(selector, k), piece(rms_norm, pal_ref, hid_ref, norm_gain_ref, rows)]
-    work += [zeros]
+    work += [selectors_back]
     for slot in range(n_slots):
         weights_slot(slot)
         if slot == 0:
@@ -624,12 +619,19 @@
         if slot == 20:
             exchange_forward(0, recv1)
     assert not work
-    weights_wait()
-    project(0, 3 * PROJ)
-    for t in pairs:
-        attend(t)
-
-    att_ref[...] = acc_ref[...].astype(BF16)
+    for port in range(2):
+
+        @pl.when(core == port)
+        def _():
+            spans = ((0, SPLIT), (SPLIT, 3 * PROJ))
+            project(*spans[port])
+            rows_wait(port_rows(1 - port), other_recv.at[0])
+            project(*spans[1 - port])
+            if port == 0:
+                rows_wait(wo_wide, other_recv.at[1])
+
+    for block in BLOCKS:
+        attend(*block)
 
     @pl.loop(0, D // 256)
     def _(i):
@@ -657,8 +659,6 @@
     send2[:, D + 256 :] = tail_part.astype(BF16)
     exchange_start(1, send2, recv2)
 
-    selectors_back()
-    dqkv_ref[...] = jnp.zeros_like(dqkv_ref)
     exchange_wait(0, send1, recv1)
 
     def gradients(rows):
@@ -691,9 +691,10 @@
     for c0, c1 in ((0, 256), (256, 512), (512, 640)):
         ag_ref[:, c0:c1] = dot_nt(rgb_ref[...], wo_ref[c0:c1, :]).astype(BF16)
 
-    for t in pairs:
-        for r0 in (0, 128):
-            rows = slice(r0, r0 + 128)
+    for r0 in (0, 128):
+        rows = slice(r0, r0 + 128)
+        carries = [None] * 3
+        for t in pairs:
             grad = ag_ref[rows, window(t)]
             values = two_heads(t, qkv_ref[rows, window(t, 2 * PROJ)])
             keys = two_heads(t, qkv_ref[rows, window(t, PROJ)])
@@ -709,11 +710,8 @@
             queries = two_heads(t, qkv_ref[rows, window(t)])
             dk = dot_tn(jnp.concatenate(score_grads, 0), queries)
             dv = dot_tn(jnp.concatenate(probs, 0), two_heads(t, grad))
-            dqkv_ref[rows, window(t)] += dq
-            dqkv_ref[rows, window(t, PROJ)] += dk
-            dqkv_ref[rows, window(t, 2 * PROJ)] += dv
-
-    dqkvb_ref[...] = dqkv_ref[...].astype(BF16)
+            for k, value in enumerate((dq, dk, dv)):
+                carries[k] = join(dqkvb_ref, rows, k * PROJ, t, value, carries[k])
 
     @pl.loop(0, D // 256)
     def _(i):
@@ -745,20 +743,23 @@
 
 
 def place_kernel(n_enc, slabs_ref, grads_ref, llm_ref, pg_ref, wide_ref, llm_wide):
-    for t in range(SLAB_W // 128):
-        wide_ref[t] = slabs_ref[:, 128 * t : 128 * t + 128].astype(F32)
-    for q in range(4):
-        for t in range(D // 128):
-            at = q * (D // 128) + t
-            for slot in range(4):
-                part = wide_ref[t, pl.ds(4 * slot + q, n_enc, stride=SLAB), :]
-                llm_wide[at, pl.ds(slot, n_enc, stride=CAP), :] = part
-        for p, (off, width) in enumerate(PIECES):
-            for t in range(width // 128):
-                at = (q * D + off) // 128 + t
-                part = wide_ref[D // 128 + t, pl.ds(4 * q + p, n_enc, stride=SLAB), :]
-                llm_wide[at, pl.ds(4, n_enc, stride=CAP), :] = part
-    for t in range(4 * D // 128):
+    q = pl.program_id(0)
+
+    @pl.when(q == 0)
+    def _():
+        for t in range(SLAB_W // 128):
+            wide_ref[t] = slabs_ref[:, 128 * t : 128 * t + 128].astype(F32)
+
+    n_tile = D // 128
+    for t in range(n_tile):
+        for slot in range(4):
+            part = wide_ref[t, pl.ds(4 * slot + q, n_enc, stride=SLAB), :]
+            llm_wide[t, pl.ds(slot, n_enc, stride=CAP), :] = part
+    for p, (off, width) in enumerate(PIECES):
+        for t in range(width // 128):
+            part = wide_ref[n_tile + t, pl.ds(4 * q + p, n_enc, stride=SLAB), :]
+            llm_wide[off // 128 + t, pl.ds(4, n_enc, stride=CAP), :] = part
+    for t in range(n_tile):
         llm_ref[:, 128 * t : 128 * t + 128] = llm_wide[t].astype(BF16)
     pg_ref[...] = grads_ref[...]
 
@@ -807,7 +808,6 @@
             pltpu.VMEM((AL, 3 * PROJ), BF16),
             pltpu.VMEM((HEADS, ROWS, 128), F32),
             pltpu.VMEM((AL, 128), F32),
-            pltpu.VMEM((AL, PROJ), F32),
             pltpu.VMEM((AL, PROJ), BF16),
             pltpu.VMEM((AL, D), BF16),
             pltpu.VMEM((AL, D), BF16),
@@ -816,7 +816,6 @@
             pltpu.VMEM((ROWS, D), F32),
             pltpu.VMEM((ROWS, D), BF16),
             pltpu.VMEM((ROWS, PROJ), BF16),
-            pltpu.VMEM((ROWS, 3 * PROJ), F32),
             pltpu.VMEM((ROWS, 3 * PROJ), BF16),
             pltpu.VMEM((ROWS, D), F32),
             pltpu.VMEM((ROWS, D), BF16),
@@ -865,11 +864,18 @@
             jax.ShapeDtypeStruct((n_slot, 4 * D), BF16),
             jax.ShapeDtypeStruct((ROWS, D), BF16),
         ),
-        in_specs=[vmem, vmem],
-        out_specs=(vmem, vmem),
+        grid=(4,),
+        in_specs=[
+            pl.BlockSpec((n_enc * SLAB, SLAB_W), lambda q: (0, 0)),
+            pl.BlockSpec((WIN, D), lambda q: (q, 0)),
+        ],
+        out_specs=(
+            pl.BlockSpec((n_slot, D), lambda q: (0, q)),
+            pl.BlockSpec((WIN, D), lambda q: (q, 0)),
+        ),
         scratch_shapes=[
             pltpu.VMEM((SLAB_W // 128, n_enc * SLAB, 128), F32),
-            pltpu.VMEM((4 * D // 128, n_slot, 128), F32),
+            pltpu.VMEM((D // 128, n_slot, 128), F32),
         ],
         compiler_params=pltpu.CompilerParams(vmem_limit_bytes=60 * 1024 * 1024),
         cost_estimate=pl.CostEstimate(

time: 84.3 us -> 85.9 us (1.019)
  Pallas kernels: 83.5 us -> 85.1 us
    pallas_call x1, Pallas kernels: 3.23 us -> 4.12 us  [per_device(): pl.pallas_call(functools.partial(place_kernel, n_enc), out_shape=(jax.Sha...]
where the time goes in v2:
time: 85.9 us; the launch traced here: 85.7 us
  Pallas kernels  85.1 us (99%)
    pallas_call x1, Pallas kernels, per_device(): pl.pallas_call(functools.partial(kernel, n_enc, n_x, n_z), out_shape=(jax...  81 us
    pallas_call x1, Pallas kernels, per_device(): pl.pallas_call(functools.partial(place_kernel, n_enc), out_shape=(jax.Sha...  4.12 us

profile of v2, /device:TPU:1, one launch (start us, length us, event | category | flops | bytes accessed | tf_op | source)
XLA Modules:
  0.0 85.7 jit_solution(5964993462660311845)
XLA Ops:
  0.6 81.0 %shard_map.104 = (bf16[256,1664]{1,0:T(8,128)(2,1)}, bf16[256,1280]{1,0:T(8,128)(2,1)}) custom-call(s32[16]{0:T(128)} %phase_ref.1, bf16[256,1280]{1,0:T(8,128)(2,1)} %patches_hbm.1, f32[1280]{0:T(1024)} %norm_gain_ref.1, f32[1280]{0:T(1024)} %merge_gain_ref.1, bf16[40,1920]{1,0:T(8,128)(2,1)} %qkv_shard_ref.1, bf16[20,1280]{1,0:T(8,128)(2,1)} %out_shard_ref.1, ...), custom_call_target="tpu_custom_call" | custom-call | flops 8000000000 | bytes 4000000 | tf_op jit(solution)/shard_map/pallas_call | solution.py:788
  81.6 4.1 %shard_map.105 = (bf16[80,5120]{1,0:T(8,128)(2,1)}, bf16[256,1280]{1,0:T(8,128)(2,1)}) custom-call(bf16[256,1664]{1,0:T(8,128)(2,1)} %get-tuple-element.4.slabs_ref, bf16[256,1280]{1,0:T(8,128)(2,1)} %get-tuple-element.5.grads_ref), custom_call_target="tpu_custom_call" | custom-call | flops 1000000 | bytes 3200000 | tf_op jit(solution)/shard_map/pallas_call | solution.py:861

commit v3 on v2

--- a/solution.py
+++ b/solution.py
@@ -172,6 +172,7 @@
     forward_send,
     own_sem,
     fetch_sem,
+    ready_sem,
 ):
     n_row = n_x * n_z
     n_y = n_enc // 2
@@ -208,16 +209,34 @@
     fetch_grads.start()
 
     barrier = pltpu.get_barrier_semaphore()
-    peers = [(enc, xz(1, 0)), (enc, xz(-1, 0)), (enc, xz(0, 1)), (enc, xz(0, -1))]
-    peers += [(enc, left), (enc, right)]
-    for peer in peers:
-        pl.semaphore_signal(barrier, inc=1, device_id=peer, device_id_type=MESH)
+    above = [xz(0, 1), right]
+    below_z = [xz(0, -1), left]
+
+    def tell(sem, target):
+        pl.semaphore_signal(sem, inc=1, device_id=(enc, target), device_id_type=MESH)
+
+    for target in (xz(1, 0), xz(-1, 0)):
+        tell(barrier, target)
 
     @pl.loop(1, n_enc)
     def _(d):
         pl.semaphore_signal(
             barrier, inc=1, device_id=(lax.rem(enc + d, n_enc), row), device_id_type=MESH
         )
+
+    def tell_neighbours(sem, higher):
+        @pl.when((z < n_z - 1) if higher else (z == n_z - 1))
+        def _():
+            for target in above:
+                tell(sem, target)
+
+        @pl.when((z == 0) if higher else (z > 0))
+        def _():
+            for target in below_z:
+                tell(sem, target)
+
+    tell_neighbours(barrier, True)
+    n_lower = jnp.where(z == 0, 0, jnp.where(z == n_z - 1, 4, 2))
 
     q_wide = qkv_shard_ref[...].astype(F32)
     odd_z = lax.rem(z, 2)
@@ -240,7 +259,6 @@
     wg0[row] = stacked(q_wide[:, :512], q_wide[:, 512:SPLIT])
     wg1[row] = stacked(q_wide[:, SPLIT:1792], jnp.concatenate([q_wide[:, 1792:], out40], 1))
 
-    pl.semaphore_wait(barrier, len(peers) + n_enc - 1)
 
     plans = ring_plan(n_x, n_z)
     bufs = (wg0, wg1)
@@ -479,11 +497,9 @@
                     part = jnp.zeros((n_enc, 128), F32)
                 slab_wide[n_tile + t, pl.ds(4 * q + p, n_enc, stride=SLAB), :] = part
 
-    def grads_pack(first, last):
-        for t in range(first, last):
+    def grads_pack():
+        for t in range(SLAB_W // 128):
             send1[:, 128 * t : 128 * t + 128] = slab_wide[t].astype(BF16)
-        if last == SLAB_W // 128:
-            exchange_start(0, send1, recv1)
 
     n_tok = ROWS // 4
 
@@ -601,10 +617,20 @@
             values = two_heads(t, qkv_ref[keys, window(t, 2 * PROJ)])
             carry = join(att_ref, rows, 0, t, dot(jnp.concatenate(both, 1), values), carry)
 
-    work = [piece(grads_wide, 0, 2), piece(grads_wide, 2, 4)]
-    work += [piece(grads_move, q) for q in range(4)]
-    work += [piece(grads_pack, 0, SLAB_W // 128)]
-    work += [piece(masks, *block) for block in BLOCKS]
+    grads_wide(0, 4)
+    for q in range(4):
+        grads_move(q)
+    grads_pack()
+    pl.semaphore_wait(barrier, n_enc + 1 + n_lower)
+    tell_neighbours(ready_sem, False)
+    exchange_start(0, send1, recv1)
+
+    @pl.when(z < n_z - 1)
+    def _():
+        pl.semaphore_wait(ready_sem, 4 - n_lower)
+
+
+    work = [piece(masks, *block) for block in BLOCKS]
     work += [rims_in, selector_targets]
     for k in range(5):
         rows = slice(k * WIN, (k + 1) * WIN)
@@ -743,23 +769,20 @@
 
 
 def place_kernel(n_enc, slabs_ref, grads_ref, llm_ref, pg_ref, wide_ref, llm_wide):
-    q = pl.program_id(0)
-
-    @pl.when(q == 0)
-    def _():
-        for t in range(SLAB_W // 128):
-            wide_ref[t] = slabs_ref[:, 128 * t : 128 * t + 128].astype(F32)
-
-    n_tile = D // 128
-    for t in range(n_tile):
-        for slot in range(4):
-            part = wide_ref[t, pl.ds(4 * slot + q, n_enc, stride=SLAB), :]
-            llm_wide[t, pl.ds(slot, n_enc, stride=CAP), :] = part
-    for p, (off, width) in enumerate(PIECES):
-        for t in range(width // 128):
-            part = wide_ref[n_tile + t, pl.ds(4 * q + p, n_enc, stride=SLAB), :]
-            llm_wide[off // 128 + t, pl.ds(4, n_enc, stride=CAP), :] = part
-    for t in range(n_tile):
+    for t in range(SLAB_W // 128):
+        wide_ref[t] = slabs_ref[:, 128 * t : 128 * t + 128].astype(F32)
+    for q in range(4):
+        for t in range(D // 128):
+            at = q * (D // 128) + t
+            for slot in range(4):
+                part = wide_ref[t, pl.ds(4 * slot + q, n_enc, stride=SLAB), :]
+                llm_wide[at, pl.ds(slot, n_enc, stride=CAP), :] = part
+        for p, (off, width) in enumerate(PIECES):
+            for t in range(width // 128):
+                at = (q * D + off) // 128 + t
+                part = wide_ref[D // 128 + t, pl.ds(4 * q + p, n_enc, stride=SLAB), :]
+                llm_wide[at, pl.ds(4, n_enc, stride=CAP), :] = part
+    for t in range(4 * D // 128):
         llm_ref[:, 128 * t : 128 * t + 128] = llm_wide[t].astype(BF16)
     pg_ref[...] = grads_ref[...]
 
@@ -842,6 +865,7 @@
             dma((2,)),
             dma((2,)),
             dma((2,)),
+            pltpu.SemaphoreType.REGULAR,
         ],
         compiler_params=pltpu.CompilerParams(
             collective_id=0, has_side_effects=True, vmem_limit_bytes=56 * 1024 * 1024
@@ -864,18 +888,11 @@
             jax.ShapeDtypeStruct((n_slot, 4 * D), BF16),
             jax.ShapeDtypeStruct((ROWS, D), BF16),
         ),
-        grid=(4,),
-        in_specs=[
-            pl.BlockSpec((n_enc * SLAB, SLAB_W), lambda q: (0, 0)),
-            pl.BlockSpec((WIN, D), lambda q: (q, 0)),
-        ],
-        out_specs=(
-            pl.BlockSpec((n_slot, D), lambda q: (0, q)),
-            pl.BlockSpec((WIN, D), lambda q: (q, 0)),
-        ),
+        in_specs=[vmem, vmem],
+        out_specs=(vmem, vmem),
         scratch_shapes=[
             pltpu.VMEM((SLAB_W // 128, n_enc * SLAB, 128), F32),
-            pltpu.VMEM((D // 128, n_slot, 128), F32),
+            pltpu.VMEM((4 * D // 128, n_slot, 128), F32),
         ],
         compiler_params=pltpu.CompilerParams(vmem_limit_bytes=60 * 1024 * 1024),
         cost_estimate=pl.CostEstimate(

time: 85.9 us -> 87.4 us (1.017)
  Pallas kernels: 85.1 us -> 86.6 us
    pallas_call x1, Pallas kernels: 81 us -> 83.4 us  [per_device(): pl.pallas_call(functools.partial(kernel, n_enc, n_x, n_z), out_shape=(jax...]
    pallas_call x1, Pallas kernels: 4.12 us -> 3.23 us  [per_device(): pl.pallas_call(functools.partial(place_kernel, n_enc), out_shape=(jax.Sha...]
where the time goes in v3:
time: 87.4 us; the launch traced here: 87.2 us
  Pallas kernels  86.6 us (99%)
    pallas_call x1, Pallas kernels, per_device(): pl.pallas_call(functools.partial(kernel, n_enc, n_x, n_z), out_shape=(jax...  83.4 us
    pallas_call x1, Pallas kernels, per_device(): pl.pallas_call(functools.partial(place_kernel, n_enc), out_shape=(jax.Sha...  3.23 us

profile of v3, /device:TPU:1, one launch (start us, length us, event | category | flops | bytes accessed | tf_op | source)
XLA Modules:
  0.0 87.2 jit_solution(5108724049970409060)
XLA Ops:
  0.6 83.4 %shard_map.104 = (bf16[256,1664]{1,0:T(8,128)(2,1)}, bf16[256,1280]{1,0:T(8,128)(2,1)}) custom-call(s32[16]{0:T(128)} %phase_ref.1, bf16[256,1280]{1,0:T(8,128)(2,1)} %patches_hbm.1, f32[1280]{0:T(1024)} %norm_gain_ref.1, f32[1280]{0:T(1024)} %merge_gain_ref.1, bf16[40,1920]{1,0:T(8,128)(2,1)} %qkv_shard_ref.1, bf16[20,1280]{1,0:T(8,128)(2,1)} %out_shard_ref.1, ...), custom_call_target="tpu_custom_call" | custom-call | flops 8000000000 | bytes 4000000 | tf_op jit(solution)/shard_map/pallas_call | solution.py:811
  84.0 3.2 %shard_map.105 = (bf16[80,5120]{1,0:T(8,128)(2,1)}, bf16[256,1280]{1,0:T(8,128)(2,1)}) custom-call(bf16[256,1664]{1,0:T(8,128)(2,1)} %get-tuple-element.4.slabs_ref, bf16[256,1280]{1,0:T(8,128)(2,1)} %get-tuple-element.5.grads_ref), custom_call_target="tpu_custom_call" | custom-call | flops 1000000 | bytes 3200000 | tf_op jit(solution)/shard_map/pallas_call | solution.py:885

commit v4 on v2

--- a/solution.py
+++ b/solution.py
@@ -160,6 +160,7 @@
     send2,
     relay1,
     relay2,
+    stage,
     w_send,
     w_recv,
     other_recv,
@@ -172,6 +173,8 @@
     forward_send,
     own_sem,
     fetch_sem,
+    bundle_send,
+    bundle_recv,
 ):
     n_row = n_x * n_z
     n_y = n_enc // 2
@@ -388,17 +391,36 @@
             device_id_type=MESH,
         )
 
-    def near_peers():
-        for o in range(n_y // 2 - 1, 0, -1):
-            ahead, behind = chip(o), chip(-o)
-            for side in (0, 1):
-                turned = ahead + (behind - ahead) * (core if side == 0 else 1 - core)
-                for k in range(2):
-                    yield 2 * turned + k
-        yield sibling
+    half = n_y // 2
+
+    def bundle(ref, c):
+        return ref.at[pl.ds(pl.multiple_of(2 * SLAB * c, 2 * SLAB), 2 * SLAB)]
+
+    def bundle_copies(index, send):
+        for d in range(half - 1, 0, -1):
+            up, down = chip(d), chip(-d)
+            for side in range(2):
+                turned = core if side == 0 else 1 - core
+                target = up + (down - up) * turned
+                yield pltpu.make_async_remote_copy(
+                    src_ref=bundle(send, target),
+                    dst_ref=stage.at[index, 2 * (half - 1 - d) + turned],
+                    send_sem=bundle_send.at[index],
+                    recv_sem=bundle_recv.at[index, 0 if d > 1 else 1],
+                    device_id=(2 * target + core, row),
+                    device_id_type=MESH,
+                )
+
+    n_stage = 2 * half - 1
+    groups = (range(0, n_stage - 3), range(n_stage - 3, n_stage))
+
+    def origin_of(b):
+        if b == n_stage - 1:
+            return chip(half)
+        d = half - 1 - b // 2
+        return chip(-d if b % 2 == 0 else d)
 
     next_chip = chip(1) + (chip(-1) - chip(1)) * core
-    last_chip = chip(-1) + (chip(1) - chip(-1)) * core
     far_chip = chip(n_y // 2 - 1) + (chip(n_y // 2 + 1) - chip(n_y // 2 - 1)) * core
 
     def relay_copy(index, send):
@@ -412,14 +434,13 @@
             device_id_type=MESH,
         )
 
-    def forward_copy(index, recv, k):
-        origin = 2 * last_chip + core
+    def forward_copy(index):
         return pltpu.make_async_remote_copy(
-            src_ref=(relay1, relay2)[index].at[pl.ds(SLAB * k, SLAB)],
-            dst_ref=slab(recv, origin),
+            src_ref=(relay1, relay2)[index],
+            dst_ref=stage.at[index, n_stage - 1],
             send_sem=forward_send.at[index],
-            recv_sem=slab_recv.at[index],
-            device_id=(2 * far_chip + k, row),
+            recv_sem=bundle_recv.at[index, 1],
+            device_id=(2 * far_chip + core, row),
             device_id_type=MESH,
         )
 
@@ -428,22 +449,45 @@
 
     def exchange_start(index, send, recv):
         relay_copy(index, send).start()
-        for peer in near_peers():
-            exchange_copy(index, send, recv, peer).start()
+        for copy in bundle_copies(index, send):
+            copy.start()
+        exchange_copy(index, send, recv, sibling).start()
         own_copy(index, send, recv).start()
 
-    def exchange_forward(index, recv):
+    def exchange_forward(index):
         relay_copy(index, send1).wait_recv()
-        for k in range(2):
-            forward_copy(index, recv, k).start()
-
-    def exchange_wait(index, send, recv):
-        own_copy(index, send, recv).wait()
-        rows_wait(recv.at[pl.ds(0, (n_enc - 1) * SLAB)], slab_recv.at[index])
+        forward_copy(index).start()
+
+    def exchange_collect(index, recv, group):
+        first = groups[group].start
+        here = stage.at[index, pl.ds(first, len(groups[group]))]
+        rows_wait(here, bundle_recv.at[index, group])
+        for b in groups[group]:
+            origin = 2 * origin_of(b) + core
+
+            def part(c):
+                return stage.at[index, b, pl.ds(pl.multiple_of(SLAB * c, SLAB), SLAB)]
+
+            pltpu.make_async_remote_copy(
+                src_ref=part(1 - core),
+                dst_ref=slab(recv, origin),
+                send_sem=slab_send.at[index],
+                recv_sem=slab_recv.at[index],
+                device_id=(sibling, row),
+                device_id_type=MESH,
+            ).start()
+            pltpu.make_async_copy(part(core), slab(recv, origin), own_sem.at[index]).start()
+
+    half_rows = pl.ds(0, n_y * SLAB)
+
+    def exchange_wait(index, recv):
+        rows_wait(recv.at[half_rows], own_sem.at[index])
+        rows_wait(recv.at[half_rows], slab_recv.at[index])
 
     def exchange_drain(index, send):
         relay_copy(index, send).wait_send()
-        rows_wait(send.at[pl.ds(0, (n_enc - 3) * SLAB)], slab_send.at[index])
+        rows_wait(send.at[pl.ds(0, 2 * SLAB * (n_stage - 1))], bundle_send.at[index])
+        rows_wait(send.at[half_rows], slab_send.at[index])
         rows_wait((relay1, relay2)[index], forward_send.at[index])
 
     def rotate():
@@ -617,7 +661,7 @@
         elif work:
             work.pop(0)()
         if slot == 20:
-            exchange_forward(0, recv1)
+            exchange_forward(0)
     assert not work
     for port in range(2):
 
@@ -659,7 +703,9 @@
     send2[:, D + 256 :] = tail_part.astype(BF16)
     exchange_start(1, send2, recv2)
 
-    exchange_wait(0, send1, recv1)
+    exchange_collect(0, recv1, 0)
+    exchange_collect(0, recv1, 1)
+    exchange_wait(0, recv1)
 
     def gradients(rows):
         for p, (off, width) in enumerate(PIECES):
@@ -686,7 +732,7 @@
     ng_rim.wait()
     merge_back(slice(0, WIN), jnp.where(below, ng_rim_ref[...], ng_ref[:WIN, :]))
 
-    exchange_forward(1, recv2)
+    exchange_forward(1)
 
     for c0, c1 in ((0, 256), (256, 512), (512, 640)):
         ag_ref[:, c0:c1] = dot_nt(rgb_ref[...], wo_ref[c0:c1, :]).astype(BF16)
@@ -729,6 +775,7 @@
     def _(i):
         norm_back(pl.ds(pl.multiple_of(i * WIN, WIN), WIN))
 
+    exchange_collect(1, recv2, 0)
     grad_rim.wait()
     own_ref[:WIN, :] = jnp.where(below, grad_rim_ref[...], pal_grad_ref[:WIN, :])
     own_ref[WIN:, :] = pal_grad_ref[WIN:, :]
@@ -738,28 +785,26 @@
 
     exchange_drain(0, send1)
     weights_drain()
+    exchange_collect(1, recv2, 1)
     exchange_drain(1, send2)
-    exchange_wait(1, send2, recv2)
+    exchange_wait(1, recv2)
 
 
 def place_kernel(n_enc, slabs_ref, grads_ref, llm_ref, pg_ref, wide_ref, llm_wide):
-    q = pl.program_id(0)
-
-    @pl.when(q == 0)
-    def _():
-        for t in range(SLAB_W // 128):
-            wide_ref[t] = slabs_ref[:, 128 * t : 128 * t + 128].astype(F32)
-
-    n_tile = D // 128
-    for t in range(n_tile):
-        for slot in range(4):
-            part = wide_ref[t, pl.ds(4 * slot + q, n_enc, stride=SLAB), :]
-            llm_wide[t, pl.ds(slot, n_enc, stride=CAP), :] = part
-    for p, (off, width) in enumerate(PIECES):
-        for t in range(width // 128):
-            part = wide_ref[n_tile + t, pl.ds(4 * q + p, n_enc, stride=SLAB), :]
-            llm_wide[off // 128 + t, pl.ds(4, n_enc, stride=CAP), :] = part
-    for t in range(n_tile):
+    for t in range(SLAB_W // 128):
+        wide_ref[t] = slabs_ref[:, 128 * t : 128 * t + 128].astype(F32)
+    for q in range(4):
+        for t in range(D // 128):
+            at = q * (D // 128) + t
+            for slot in range(4):
+                part = wide_ref[t, pl.ds(4 * slot + q, n_enc, stride=SLAB), :]
+                llm_wide[at, pl.ds(slot, n_enc, stride=CAP), :] = part
+        for p, (off, width) in enumerate(PIECES):
+            for t in range(width // 128):
+                at = (q * D + off) // 128 + t
+                part = wide_ref[D // 128 + t, pl.ds(4 * q + p, n_enc, stride=SLAB), :]
+                llm_wide[at, pl.ds(4, n_enc, stride=CAP), :] = part
+    for t in range(4 * D // 128):
         llm_ref[:, 128 * t : 128 * t + 128] = llm_wide[t].astype(BF16)
     pg_ref[...] = grads_ref[...]
 
@@ -830,6 +875,7 @@
             slabs,
             pltpu.VMEM((2 * SLAB, SLAB_W), BF16),
             pltpu.VMEM((2 * SLAB, SLAB_W), BF16),
+            pltpu.VMEM((2, 2 * (n_enc // 4) - 1, 2 * SLAB, SLAB_W), BF16),
             dma((3,)),
             dma((n_row,)),
             dma((2,)),
@@ -842,6 +888,8 @@
             dma((2,)),
             dma((2,)),
             dma((2,)),
+            dma((2,)),
+            dma((2, 2)),
         ],
         compiler_params=pltpu.CompilerParams(
             collective_id=0, has_side_effects=True, vmem_limit_bytes=56 * 1024 * 1024
@@ -864,18 +912,11 @@
             jax.ShapeDtypeStruct((n_slot, 4 * D), BF16),
             jax.ShapeDtypeStruct((ROWS, D), BF16),
         ),
-        grid=(4,),
-        in_specs=[
-            pl.BlockSpec((n_enc * SLAB, SLAB_W), lambda q: (0, 0)),
-            pl.BlockSpec((WIN, D), lambda q: (q, 0)),
-        ],
-        out_specs=(
-            pl.BlockSpec((n_slot, D), lambda q: (0, q)),
-            pl.BlockSpec((WIN, D), lambda q: (q, 0)),
-        ),
+        in_specs=[vmem, vmem],
+        out_specs=(vmem, vmem),
         scratch_shapes=[
             pltpu.VMEM((SLAB_W // 128, n_enc * SLAB, 128), F32),
-            pltpu.VMEM((D // 128, n_slot, 128), F32),
+            pltpu.VMEM((4 * D // 128, n_slot, 128), F32),
         ],
         compiler_params=pltpu.CompilerParams(vmem_limit_bytes=60 * 1024 * 1024),
         cost_estimate=pl.CostEstimate(

time: 85.9 us -> 86.5 us (level)
    pallas_call x1, Pallas kernels: 81 us -> 82.5 us  [per_device(): pl.pallas_call(functools.partial(kernel, n_enc, n_x, n_z), out_shape=(jax...]
    pallas_call x1, Pallas kernels: 4.12 us -> 3.23 us  [per_device(): pl.pallas_call(functools.partial(place_kernel, n_enc), out_shape=(jax.Sha...]
where the time goes in v4:
time: 86.5 us; the launch traced here: 86.4 us
  Pallas kernels  85.7 us (99%)
    pallas_call x1, Pallas kernels, per_device(): pl.pallas_call(functools.partial(kernel, n_enc, n_x, n_z), out_shape=(jax...  82.5 us
    pallas_call x1, Pallas kernels, per_device(): pl.pallas_call(functools.partial(place_kernel, n_enc), out_shape=(jax.Sha...  3.23 us

profile of v4, /device:TPU:1, one launch (start us, length us, event | category | flops | bytes accessed | tf_op | source)
XLA Modules:
  0.0 86.4 jit_solution(14845787440007788882)
XLA Ops:
  0.6 82.5 %shard_map.104 = (bf16[256,1664]{1,0:T(8,128)(2,1)}, bf16[256,1280]{1,0:T(8,128)(2,1)}) custom-call(s32[16]{0:T(128)} %phase_ref.1, bf16[256,1280]{1,0:T(8,128)(2,1)} %patches_hbm.1, f32[1280]{0:T(1024)} %norm_gain_ref.1, f32[1280]{0:T(1024)} %merge_gain_ref.1, bf16[40,1920]{1,0:T(8,128)(2,1)} %qkv_shard_ref.1, bf16[20,1280]{1,0:T(8,128)(2,1)} %out_shard_ref.1, ...), custom_call_target="tpu_custom_call" | custom-call | flops 8000000000 | bytes 4000000 | tf_op jit(solution)/shard_map/pallas_call | solution.py:833
  83.1 3.2 %shard_map.105 = (bf16[80,5120]{1,0:T(8,128)(2,1)}, bf16[256,1280]{1,0:T(8,128)(2,1)}) custom-call(bf16[256,1664]{1,0:T(8,128)(2,1)} %get-tuple-element.4.slabs_ref, bf16[256,1280]{1,0:T(8,128)(2,1)} %get-tuple-element.5.grads_ref), custom_call_target="tpu_custom_call" | custom-call | flops 1000000 | bytes 3200000 | tf_op jit(solution)/shard_map/pallas_call | solution.py:909

commit v5 on v1

--- a/solution.py
+++ b/solution.py
@@ -26,6 +26,7 @@
 SLAB_W = 1664
 PIECES = ((0, 384), (384, 384), (768, 256), (1024, 256))
 BLOCKS = ((0, 128, 0), (128, 128, 128), (256, 64, 192))
+PART = 16
 SLOT = 0.5
 
 F32 = jnp.float32
@@ -547,6 +548,7 @@
 
     def zeros():
         acc_ref[...] = jnp.zeros_like(acc_ref)
+        dqkv_ref[...] = jnp.zeros_like(dqkv_ref)
 
     below = iota((WIN, 1), 0) < edge
 
@@ -557,10 +559,17 @@
         pal_ref[WIN:ROWS, :] = own_ref[WIN:, :]
         pal_ref[ROWS:, :] = jnp.where(below, own_ref[:WIN, :], rim_ref[1])
 
-    def rms_norm(src, dst, gain_ref, rows):
-        wide = src[rows, :].astype(F32)
-        inv = lax.rsqrt(jnp.mean(wide * wide, -1, keepdims=True) + EPS)
-        dst[rows, :] = (wide * inv * gain_ref[...].reshape(1, D)).astype(BF16)
+    def in_parts(first, body):
+        for k in range(WIN // PART):
+            body(pl.ds(pl.multiple_of(first + PART * k, PART), PART))
+
+    def rms_norm(src, dst, gain_ref, first):
+        def body(rows):
+            wide = src[rows, :].astype(F32)
+            inv = lax.rsqrt(jnp.mean(wide * wide, -1, keepdims=True) + EPS)
+            dst[rows, :] = (wide * inv * gain_ref[...].reshape(1, D)).astype(BF16)
+
+        in_parts(first, body)
 
     def rms_back(wide, gain_ref, upstream_in):
         inv = lax.rsqrt(jnp.mean(wide * wide, -1, keepdims=True) + EPS)
@@ -612,9 +621,8 @@
     work += [piece(masks, *block) for block in BLOCKS]
     work += [rims_in, selector_targets]
     for k in range(5):
-        rows = slice(k * WIN, (k + 1) * WIN)
-        work += [piece(selector, k), piece(rms_norm, pal_ref, hid_ref, norm_gain_ref, rows)]
-    work += [zeros]
+        work += [piece(selector, k), piece(rms_norm, pal_ref, hid_ref, norm_gain_ref, k * WIN)]
+    work += [zeros, selectors_back]
     for slot in range(n_slots):
         weights_slot(slot)
         if slot == 0:
@@ -640,8 +648,7 @@
 
     @pl.loop(0, AL // WIN)
     def _(i):
-        rows = pl.ds(pl.multiple_of(i * WIN, WIN), WIN)
-        rms_norm(resid_ref, normed_ref, merge_gain_ref, rows)
+        rms_norm(resid_ref, normed_ref, merge_gain_ref, i * WIN)
 
     normed_ref[:WIN, :] = jnp.where(below, normed_ref[ROWS:, :], normed_ref[:WIN, :])
 
@@ -657,8 +664,6 @@
     send2[:, D + 256 :] = tail_part.astype(BF16)
     exchange_start(1, send2, recv2)
 
-    selectors_back()
-    dqkv_ref[...] = jnp.zeros_like(dqkv_ref)
     exchange_wait(0, send1, recv1)
 
     def gradients(rows):
@@ -673,18 +678,19 @@
     ng_rim.start()
     gradients(slice(WIN, ROWS))
 
-    def merge_back(rows, grad_in):
-        grad = rms_back(resid_ref[rows, :].astype(F32), merge_gain_ref, grad_in.astype(F32))
+    def merge_back(rows):
+        upstream = ng_ref[rows, :].astype(F32)
+        grad = rms_back(resid_ref[rows, :].astype(F32), merge_gain_ref, upstream)
         rg_ref[rows, :] = grad
         rgb_ref[rows, :] = grad.astype(BF16)
 
     @pl.loop(1, ROWS // WIN)
     def _(i):
-        rows = pl.ds(pl.multiple_of(i * WIN, WIN), WIN)
-        merge_back(rows, ng_ref[rows, :])
+        in_parts(i * WIN, merge_back)
 
     ng_rim.wait()
-    merge_back(slice(0, WIN), jnp.where(below, ng_rim_ref[...], ng_ref[:WIN, :]))
+    ng_ref[:WIN, :] = jnp.where(below, ng_rim_ref[...], ng_ref[:WIN, :])
+    in_parts(0, merge_back)
 
     exchange_forward(1, recv2)
 
@@ -724,12 +730,15 @@
         grad = rms_back(pal_ref[rows, :].astype(F32), norm_gain_ref, hg_ref[rows, :])
         pal_grad_ref[rows, :] = (rg_ref[rows, :] + grad).astype(BF16)
 
-    norm_back(slice(0, WIN))
+    in_parts(0, norm_back)
     grad_rim.start()
 
     @pl.loop(1, ROWS // WIN)
     def _(i):
-        norm_back(pl.ds(pl.multiple_of(i * WIN, WIN), WIN))
+        in_parts(i * WIN, norm_back)
+
+    exchange_drain(0, send1)
+    weights_drain()
 
     grad_rim.wait()
     own_ref[:WIN, :] = jnp.where(below, grad_rim_ref[...], pal_grad_ref[:WIN, :])
@@ -738,8 +747,6 @@
         part = dot_tn(turn_ref[...], own_ref[:, c : c + 256])
         pg_ref[:, c : c + 256] = part.astype(BF16)
 
-    exchange_drain(0, send1)
-    weights_drain()
     exchange_drain(1, send2)
     exchange_wait(1, send2, recv2)
 

time: 84.3 us -> 84.4 us (level)
  no operation moved by 1% of the time
where the time goes in v5:
time: 84.4 us; the launch traced here: 84.2 us
  Pallas kernels  83.6 us (99%)
    pallas_call x1, Pallas kernels, per_device(): pl.pallas_call(functools.partial(kernel, n_enc, n_x, n_z), out_shape=(jax...  80.4 us
    pallas_call x1, Pallas kernels, per_device(): pl.pallas_call(functools.partial(place_kernel, n_enc), out_shape=(jax.Sha...  3.23 us

profile of v5, /device:TPU:1, one launch (start us, length us, event | category | flops | bytes accessed | tf_op | source)
XLA Modules:
  0.0 84.2 jit_solution(10681061563590044090)
XLA Ops:
  0.6 80.4 %shard_map.104 = (bf16[256,1664]{1,0:T(8,128)(2,1)}, bf16[256,1280]{1,0:T(8,128)(2,1)}) custom-call(s32[16]{0:T(128)} %phase_ref.1, bf16[256,1280]{1,0:T(8,128)(2,1)} %patches_hbm.1, f32[1280]{0:T(1024)} %norm_gain_ref.1, f32[1280]{0:T(1024)} %merge_gain_ref.1, bf16[40,1920]{1,0:T(8,128)(2,1)} %qkv_shard_ref.1, bf16[20,1280]{1,0:T(8,128)(2,1)} %out_shard_ref.1, ...), custom_call_target="tpu_custom_call" | custom-call | flops 8000000000 | bytes 4000000 | tf_op jit(solution)/shard_map/pallas_call | solution.py:794
  81.0 3.2 %shard_map.105 = (bf16[80,5120]{1,0:T(8,128)(2,1)}, bf16[256,1280]{1,0:T(8,128)(2,1)}) custom-call(bf16[256,1664]{1,0:T(8,128)(2,1)} %get-tuple-element.4.slabs_ref, bf16[256,1280]{1,0:T(8,128)(2,1)} %get-tuple-element.5.grads_ref), custom_call_target="tpu_custom_call" | custom-call | flops 1000000 | bytes 3200000 | tf_op jit(solution)/shard_map/pallas_call | solution.py:869

commit v6 on v5

--- a/solution.py
+++ b/solution.py
@@ -139,7 +139,6 @@
     qkv_ref,
     prob_ref,
     mask_ref,
-    acc_ref,
     att_ref,
     resid_ref,
     normed_ref,
@@ -148,7 +147,6 @@
     rg_ref,
     rgb_ref,
     ag_ref,
-    dqkv_ref,
     dqkvb_ref,
     hg_ref,
     pal_grad_ref,
@@ -349,15 +347,6 @@
                 def _():
                     run_slot(port, slot)
 
-    def weights_wait():
-        for port in range(2):
-
-            @pl.when(core != port)
-            def _():
-                rows_wait(port_rows(port), other_recv.at[0])
-                if port == 1:
-                    rows_wait(wo_wide, other_recv.at[1])
-
     def weights_drain():
         blocks = pl.ds(0, n_row - 1)
         for port in range(2):
@@ -546,10 +535,6 @@
         same = ((i >> 6) == (j >> 6)) & (apart == 0)
         mask_ref[r0 : r0 + count, :] = jnp.where(same, 1.0, 0.0)
 
-    def zeros():
-        acc_ref[...] = jnp.zeros_like(acc_ref)
-        dqkv_ref[...] = jnp.zeros_like(dqkv_ref)
-
     below = iota((WIN, 1), 0) < edge
 
     def rims_in():
@@ -599,8 +584,18 @@
         second = jnp.where((lane >= HEAD_DIM) & (lane < 2 * HEAD_DIM), value, zero)
         return jnp.concatenate([first, second], 0)
 
+    def join(ref, rows, base, t, value, carry):
+        low = value[:, :128] if carry is None else value[:, :128] + carry
+        ref[rows, base + 128 * t : base + 128 * t + 128] = low.astype(BF16)
+        high = value[:, 128:]
+        if t == pairs[-1]:
+            ref[rows, base + 128 * t + 128 : base + 128 * t + 256] = high.astype(BF16)
+        return high
+
+    carried = [None] * len(BLOCKS)
+
     def attend(t):
-        for r0, count, k0 in BLOCKS:
+        for b, (r0, count, k0) in enumerate(BLOCKS):
             rows, keys = slice(r0, r0 + count), slice(k0, k0 + 128)
             scores = dot_nt(qkv_ref[rows, window(t)], two_heads(t, qkv_ref[keys, window(t, PROJ)]))
             seen = mask_ref[rows, :] > 0.5
@@ -613,7 +608,8 @@
                     prob_ref[2 * t + g, rows, :] = p
                 both.append(p.astype(BF16))
             values = two_heads(t, qkv_ref[keys, window(t, 2 * PROJ)])
-            acc_ref[rows, window(t)] += dot(jnp.concatenate(both, 1), values)
+            mixed = dot(jnp.concatenate(both, 1), values)
+            carried[b] = join(att_ref, rows, 0, t, mixed, carried[b])
 
     work = [piece(grads_wide, 0, 2), piece(grads_wide, 2, 4)]
     work += [piece(grads_move, q) for q in range(4)]
@@ -622,7 +618,7 @@
     work += [rims_in, selector_targets]
     for k in range(5):
         work += [piece(selector, k), piece(rms_norm, pal_ref, hid_ref, norm_gain_ref, k * WIN)]
-    work += [zeros, selectors_back]
+    work += [selectors_back]
     for slot in range(n_slots):
         weights_slot(slot)
         if slot == 0:
@@ -632,12 +628,20 @@
         if slot == 20:
             exchange_forward(0, recv1)
     assert not work
-    weights_wait()
-    project(0, 3 * PROJ)
+    for port in range(2):
+
+        @pl.when(core == port)
+        def _():
+            spans = ((0, SPLIT), (SPLIT, 3 * PROJ))
+            project(*spans[port])
+            rows_wait(port_rows(1 - port), other_recv.at[0])
+            project(*spans[1 - port])
+            if port == 0:
+                rows_wait(wo_wide, other_recv.at[1])
+
     for t in pairs:
         attend(t)
 
-    att_ref[...] = acc_ref[...].astype(BF16)
 
     @pl.loop(0, D // 256)
     def _(i):
@@ -697,6 +701,7 @@
     for c0, c1 in ((0, 256), (256, 512), (512, 640)):
         ag_ref[:, c0:c1] = dot_nt(rgb_ref[...], wo_ref[c0:c1, :]).astype(BF16)
 
+    carries = {}
     for t in pairs:
         for r0 in (0, 128):
             rows = slice(r0, r0 + 128)
@@ -715,11 +720,9 @@
             queries = two_heads(t, qkv_ref[rows, window(t)])
             dk = dot_tn(jnp.concatenate(score_grads, 0), queries)
             dv = dot_tn(jnp.concatenate(probs, 0), two_heads(t, grad))
-            dqkv_ref[rows, window(t)] += dq
-            dqkv_ref[rows, window(t, PROJ)] += dk
-            dqkv_ref[rows, window(t, 2 * PROJ)] += dv
-
-    dqkvb_ref[...] = dqkv_ref[...].astype(BF16)
+            for k, value in enumerate((dq, dk, dv)):
+                key = (r0, k)
+                carries[key] = join(dqkvb_ref, rows, k * PROJ, t, value, carries.get(key))
 
     @pl.loop(0, D // 256)
     def _(i):
@@ -814,7 +817,6 @@
             pltpu.VMEM((AL, 3 * PROJ), BF16),
             pltpu.VMEM((HEADS, ROWS, 128), F32),
             pltpu.VMEM((AL, 128), F32),
-            pltpu.VMEM((AL, PROJ), F32),
             pltpu.VMEM((AL, PROJ), BF16),
             pltpu.VMEM((AL, D), BF16),
             pltpu.VMEM((AL, D), BF16),
@@ -823,7 +825,6 @@
             pltpu.VMEM((ROWS, D), F32),
             pltpu.VMEM((ROWS, D), BF16),
             pltpu.VMEM((ROWS, PROJ), BF16),
-            pltpu.VMEM((ROWS, 3 * PROJ), F32),
             pltpu.VMEM((ROWS, 3 * PROJ), BF16),
             pltpu.VMEM((ROWS, D), F32),
             pltpu.VMEM((ROWS, D), BF16),

time: 84.4 us -> 85 us (level)
  no operation moved by 1% of the time
where the time goes in v6:
time: 85 us; the launch traced here: 84.9 us
  Pallas kernels  84.2 us (99%)
    pallas_call x1, Pallas kernels, per_device(): pl.pallas_call(functools.partial(kernel, n_enc, n_x, n_z), out_shape=(jax...  81 us
    pallas_call x1, Pallas kernels, per_device(): pl.pallas_call(functools.partial(place_kernel, n_enc), out_shape=(jax.Sha...  3.23 us

profile of v6, /device:TPU:1, one launch (start us, length us, event | category | flops | bytes accessed | tf_op | source)
XLA Modules:
  0.0 84.9 jit_solution(8232007541028926767)
XLA Ops:
  0.6 81.0 %shard_map.104 = (bf16[256,1664]{1,0:T(8,128)(2,1)}, bf16[256,1280]{1,0:T(8,128)(2,1)}) custom-call(s32[16]{0:T(128)} %phase_ref.1, bf16[256,1280]{1,0:T(8,128)(2,1)} %patches_hbm.1, f32[1280]{0:T(1024)} %norm_gain_ref.1, f32[1280]{0:T(1024)} %merge_gain_ref.1, bf16[40,1920]{1,0:T(8,128)(2,1)} %qkv_shard_ref.1, bf16[20,1280]{1,0:T(8,128)(2,1)} %out_shard_ref.1, ...), custom_call_target="tpu_custom_call" | custom-call | flops 8000000000 | bytes 4000000 | tf_op jit(solution)/shard_map/pallas_call | solution.py:797
  81.6 3.2 %shard_map.105 = (bf16[80,5120]{1,0:T(8,128)(2,1)}, bf16[256,1280]{1,0:T(8,128)(2,1)}) custom-call(bf16[256,1664]{1,0:T(8,128)(2,1)} %get-tuple-element.4.slabs_ref, bf16[256,1280]{1,0:T(8,128)(2,1)} %get-tuple-element.5.grads_ref), custom_call_target="tpu_custom_call" | custom-call | flops 1000000 | bytes 3200000 | tf_op jit(solution)/shard_map/pallas_call | solution.py:870

commit v7 on v5

--- a/solution.py
+++ b/solution.py
@@ -676,6 +676,7 @@
 
     gradients(slice(0, WIN))
     ng_rim.start()
+    exchange_forward(1, recv2)
     gradients(slice(WIN, ROWS))
 
     def merge_back(rows):
@@ -692,7 +693,6 @@
     ng_ref[:WIN, :] = jnp.where(below, ng_rim_ref[...], ng_ref[:WIN, :])
     in_parts(0, merge_back)
 
-    exchange_forward(1, recv2)
 
     for c0, c1 in ((0, 256), (256, 512), (512, 640)):
         ag_ref[:, c0:c1] = dot_nt(rgb_ref[...], wo_ref[c0:c1, :]).astype(BF16)

time: 84.4 us -> 84.4 us (level)
  no operation moved by 1% of the time
where the time goes in v7:
time: 84.4 us; the launch traced here: 84.2 us
  Pallas kernels  83.6 us (99%)
    pallas_call x1, Pallas kernels, per_device(): pl.pallas_call(functools.partial(kernel, n_enc, n_x, n_z), out_shape=(jax...  80.4 us
    pallas_call x1, Pallas kernels, per_device(): pl.pallas_call(functools.partial(place_kernel, n_enc), out_shape=(jax.Sha...  3.23 us

profile of v7, /device:TPU:1, one launch (start us, length us, event | category | flops | bytes accessed | tf_op | source)
XLA Modules:
  0.0 84.2 jit_solution(15462415205469375475)
XLA Ops:
  0.6 80.4 %shard_map.104 = (bf16[256,1664]{1,0:T(8,128)(2,1)}, bf16[256,1280]{1,0:T(8,128)(2,1)}) custom-call(s32[16]{0:T(128)} %phase_ref.1, bf16[256,1280]{1,0:T(8,128)(2,1)} %patches_hbm.1, f32[1280]{0:T(1024)} %norm_gain_ref.1, f32[1280]{0:T(1024)} %merge_gain_ref.1, bf16[40,1920]{1,0:T(8,128)(2,1)} %qkv_shard_ref.1, bf16[20,1280]{1,0:T(8,128)(2,1)} %out_shard_ref.1, ...), custom_call_target="tpu_custom_call" | custom-call | flops 8000000000 | bytes 4000000 | tf_op jit(solution)/shard_map/pallas_call | solution.py:794
  81.0 3.2 %shard_map.105 = (bf16[80,5120]{1,0:T(8,128)(2,1)}, bf16[256,1280]{1,0:T(8,128)(2,1)}) custom-call(bf16[256,1664]{1,0:T(8,128)(2,1)} %get-tuple-element.4.slabs_ref, bf16[256,1280]{1,0:T(8,128)(2,1)} %get-tuple-element.5.grads_ref), custom_call_target="tpu_custom_call" | custom-call | flops 1000000 | bytes 3200000 | tf_op jit(solution)/shard_map/pallas_call | solution.py:869
